TPU v7x, 32 devices: a whole 2x2x4 slice. The times are simulated.
32 devices in a mesh: tok: 4 (over y, x), cent: 8 (over z, core).
Axes of the slice: x: 2, y: 2, z: 4, core: 2. Of those that a mesh axis runs over, the one named last changes fastest.
Arguments:
- tokens: bfloat16 [8192, 128], P('tok'), may hold values from -80 to 80
- centroids: bfloat16 [262144, 128], P('cent'), may hold values from -0.6 to 0.6
Outputs:
- updated: float32 [262144, 128], P('cent')
- masses: float32 [262144], P('cent')
All inputs are finite; a program needn't handle non-finite values.
Results may differ from a plain program's by a relative error of at most 0.0028.
Values may be sent and summed in bfloat16 or wider, within the bound.
No kernel may reach another device: no remote copies, remote signals or barrier semaphores. Data moves between devices by JAX's collectives and lax.ppermute only.
A program may use at most 128 MiB of HBM per device.

v0:
```python
import functools

import jax
import jax.numpy as jnp
from jax import lax
from jax.experimental import pallas as pl
from jax.experimental.pallas import tpu as pltpu
from jax.sharding import PartitionSpec as P

inverse_temp = 2.0
prior_weight = 0.05
safe_sum = 1e30
headroom = 60.0
code_scale = 2.0**24
slice_rows = 64
vmem_bytes = 56 * 1024 * 1024


def divisor(count, most):
    size = min(count, most)
    while count % size:
        size //= 2
    return size


def dot_nt(a, b):
    return lax.dot_general(a, b, (((1,), (1,)), ((), ())), preferred_element_type=jnp.float32)


def fold_rows(x, combine):
    parts = [x[k * 8 : (k + 1) * 8, :] for k in range(x.shape[0] // 8)]
    while len(parts) > 1:
        half = len(parts) // 2
        parts = [combine(parts[2 * k], parts[2 * k + 1]) for k in range(half)] + parts[2 * half :]
    return parts[0]


def stats_kernel(
    sub_rows, tok_cols, tok_ref, cent_ref, out_ref, flip_ref, base_ref, shift_ref, sums_ref, worst_ref
):
    step = pl.program_id(0)
    tok_count = tok_ref.shape[0]
    subs = cent_ref.shape[0] // sub_rows
    col_blocks = tok_count // tok_cols
    redo_cols = divisor(tok_cols, 256)
    redo_blocks = tok_count // redo_cols

    def columns(t, size=tok_cols):
        return pl.ds(pl.multiple_of(t * size, size), size)

    def dot(a, b):
        return jnp.dot(a, b, preferred_element_type=jnp.float32)

    @pl.when(step == 0)
    def _():
        @pl.loop(0, col_blocks)
        def _(t):
            flipped = (tok_ref[columns(t), :] * jnp.bfloat16(inverse_temp)).T
            flip_ref[:, columns(t)] = flipped
            logits = dot(cent_ref[0:128, :], flipped)
            top = jnp.max(fold_rows(logits, jnp.maximum), axis=0, keepdims=True)
            base_ref[:, columns(t)] = top + headroom

    @pl.loop(0, col_blocks)
    def _(t):
        rhs = flip_ref[:, columns(t)]
        shift = base_ref[:, columns(t)]
        for sub in range(subs):
            total = jnp.zeros((8, tok_cols), jnp.float32)
            logits = dot(cent_ref[pl.ds(sub * sub_rows, sub_rows), :], rhs)
            for first in range(0, sub_rows, slice_rows):
                scaled = jnp.exp(logits[first : first + slice_rows] - shift)
                total = total + fold_rows(scaled, jnp.add)
            sums_ref[step * subs + sub, :, columns(t)] = total
            shift_ref[step * subs + sub, :, columns(t)] = shift

    worst = jnp.float32(0.0)
    for sub in range(subs):
        for t in range(redo_blocks):
            block = jnp.max(sums_ref[step * subs + sub, :, t * redo_cols : (t + 1) * redo_cols])
            worst_ref[sub * redo_blocks + t] = block
            worst = jnp.maximum(worst, block)

    @pl.when(jnp.logical_not(worst < safe_sum))
    def _():
        @pl.loop(0, subs * redo_blocks)
        def _(k):
            @pl.when(jnp.logical_not(worst_ref[k] < safe_sum))
            def _():
                sub, t = k // redo_blocks, lax.rem(k, redo_blocks)
                first = pl.multiple_of(sub * sub_rows, sub_rows)
                logits = dot(cent_ref[pl.ds(first, sub_rows), :], flip_ref[:, columns(t, redo_cols)])
                top = jnp.max(fold_rows(logits, jnp.maximum), axis=0, keepdims=True)
                total = fold_rows(jnp.exp(logits - top), jnp.add)
                sums_ref[step * subs + sub, :, columns(t, redo_cols)] = total
                shift_ref[step * subs + sub, :, columns(t, redo_cols)] = top

    @pl.when(step == pl.num_programs(0) - 1)
    def _():
        @pl.loop(0, col_blocks)
        def _(t):
            shifts = shift_ref[:, :, columns(t)]
            top = jnp.max(shifts, axis=0)
            scale = jnp.exp(shifts - top[None])
            total = jnp.sum(sums_ref[:, :, columns(t)] * scale, axis=0)
            total = jnp.sum(total, axis=0, keepdims=True)
            out_ref[:, :, columns(t)] = jnp.broadcast_to(
                (top + jnp.log(total))[None], (out_ref.shape[0], 1, tok_cols)
            )


def local_lse(tokens, centroids, copies):
    tok_count, width = tokens.shape
    cent_count = centroids.shape[0]
    block_rows = divisor(cent_count, 4096)
    sub_rows = divisor(block_rows, 1024)
    tok_cols = divisor(tok_count, 512)
    blocks = cent_count // block_rows
    subs = cent_count // sub_rows
    flags = block_rows // sub_rows * (tok_count // divisor(tok_cols, 256))
    return pl.pallas_call(
        functools.partial(stats_kernel, sub_rows, tok_cols),
        grid=(blocks,),
        in_specs=[
            pl.BlockSpec((tok_count, width), lambda j: (0, 0)),
            pl.BlockSpec((block_rows, width), lambda j: (j, 0)),
        ],
        out_specs=pl.BlockSpec((copies, 1, tok_count), lambda j: (0, 0, 0)),
        out_shape=jax.ShapeDtypeStruct((copies, 1, tok_count), jnp.float32),
        scratch_shapes=[
            pltpu.VMEM((width, tok_count), jnp.bfloat16),
            pltpu.VMEM((1, tok_count), jnp.float32),
            pltpu.VMEM((subs, 1, tok_count), jnp.float32),
            pltpu.VMEM((subs, 8, tok_count), jnp.float32),
            pltpu.SMEM((flags,), jnp.float32),
        ],
        compiler_params=pltpu.CompilerParams(vmem_limit_bytes=vmem_bytes),
        cost_estimate=pl.CostEstimate(
            flops=2 * tok_count * cent_count * width,
            bytes_accessed=(tok_count + cent_count) * width * 2,
            transcendentals=tok_count * cent_count,
        ),
        name="row_stats",
    )(tokens, centroids)


def encoded(x):
    x = x * code_scale
    return (x * jnp.abs(x) * (x * x)).astype(jnp.bfloat16)


def decoded(code):
    code = code.astype(jnp.float32)
    size = lax.rsqrt(lax.rsqrt(jnp.maximum(jnp.abs(code), 1e-37))) * (1.0 / code_scale)
    return jnp.where(code < 0, -size, jnp.where(code > 0, size, 0.0))


def split_exactly(x):
    high = x.astype(jnp.bfloat16).astype(jnp.float32)
    middle = (x - high).astype(jnp.bfloat16).astype(jnp.float32)
    return high, middle, x - high - middle


class Placing:
    def __init__(self, block_rows, starts_ref, pieces, code_refs, outs, scratch):
        self.block_rows, self.starts_ref = block_rows, starts_ref
        self.pieces, self.code_refs = pieces, code_refs
        self.updated_ref, self.masses_ref = outs
        self.codes, self.values, self.masses, self.sems = scratch

    @staticmethod
    def scratch(sources, blocks, block_rows, width):
        return [
            pltpu.VMEM((sources, blocks * coded_rows(block_rows), width), jnp.bfloat16),
            pltpu.VMEM((sources, blocks * block_rows, width), jnp.float32),
            pltpu.VMEM((sources, blocks * block_rows // 128, 128), jnp.float32),
            pltpu.SemaphoreType.DMA((4, sources)),
        ]

    def copies_in(self):
        found, refs = [], list(self.code_refs)
        for s, count in enumerate(self.pieces):
            found.append([])
            first = 0
            for k in range(count):
                ref = refs.pop(0)
                target = self.codes.at[s, pl.ds(first, ref.shape[0]), :]
                found[s].append(pltpu.make_async_copy(ref, target, self.sems.at[3 * k, s]))
                first += ref.shape[0]
        return found

    def copies_out(self, s):
        rows, mass_rows = self.values.shape[1], self.masses.shape[1]
        start = self.starts_ref[s]
        span = pl.ds(pl.multiple_of(start * self.block_rows, self.block_rows), rows)
        per_block = self.block_rows // 128
        mass_span = pl.ds(pl.multiple_of(start * per_block, per_block), mass_rows)
        return [
            pltpu.make_async_copy(self.values.at[s], self.updated_ref.at[span, :], self.sems.at[1, s]),
            pltpu.make_async_copy(self.masses.at[s], self.masses_ref.at[mass_span, :], self.sems.at[2, s]),
        ]

    def fetch(self):
        for copies in self.copies_in():
            for copy in copies:
                copy.start()

    def place(self):
        block_rows, per_block = self.block_rows, self.block_rows // 128
        full = coded_rows(block_rows)
        tile = divisor(block_rows, 256)
        for s, copies in enumerate(self.copies_in()):
            for copy in copies:
                copy.wait()

            @pl.loop(0, self.values.shape[1] // block_rows)
            def _(b):
                for k in range(block_rows // tile):
                    source = pl.ds(pl.multiple_of(b * full + k * tile, 32), tile)
                    target = pl.ds(pl.multiple_of(b * block_rows + k * tile, tile), tile)
                    self.values[s, target, :] = decoded(self.codes[s, source, :])
                last = pl.ds(pl.multiple_of(b * full + block_rows, 32), full - block_rows)
                terms = self.codes[s, last, :].astype(jnp.float32)
                mass = terms[:per_block] + terms[per_block : 2 * per_block]
                mass = mass + terms[2 * per_block : 3 * per_block]
                self.masses[s, pl.ds(pl.multiple_of(b * per_block, per_block), per_block), :] = mass

            for copy in self.copies_out(s):
                copy.start()

    def finish(self):
        for s in range(len(self.pieces)):
            for copy in self.copies_out(s):
                copy.wait()


def coded_rows(block_rows):
    return block_rows + block_rows // 32


def update_kernel(unread, pieces, block_rows, *refs):
    place_ref, tok_ref, lse_ref, cent_ref = refs[:4]
    refs = refs[4 + unread :]
    code_refs, refs = refs[: sum(pieces)], refs[sum(pieces) :]
    if pieces:
        code_ref, updated_ref, masses_ref = refs[2:5]
        scratch = refs[5:]
        starts_ref = place_ref.at[pl.ds(1, len(pieces))]
        placing = Placing(
            block_rows, starts_ref, pieces, code_refs, (updated_ref, masses_ref), scratch[8:]
        )
    else:
        code_ref, scratch, placing = refs[0], refs[1:], None
    toks_ref, lses_ref, cents_ref, codes_ref, weights_ref, total_ref, mass_ref, sems = scratch[:8]
    rows, width = cents_ref.shape
    _, tile, depth = weights_ref.shape
    piece = divisor(depth, 512)
    stages = toks_ref.shape[0] // depth
    full = coded_rows(block_rows)
    per_block = block_rows // tile

    first_row = pl.multiple_of(place_ref[0] * block_rows, block_rows)
    loads = [
        pltpu.make_async_copy(cent_ref.at[pl.ds(first_row, rows), :], cents_ref, sems.at[0]),
        pltpu.make_async_copy(lse_ref, lses_ref, sems.at[1]),
    ]
    for stage in range(stages):
        span = pl.ds(stage * depth, depth)
        loads.append(pltpu.make_async_copy(tok_ref.at[span, :], toks_ref.at[span, :], sems.at[2 + stage]))
    for load in loads:
        load.start()
    if placing:
        placing.fetch()

    def weigh(first, stage):
        cents = cents_ref[pl.ds(first, tile), :] * jnp.bfloat16(inverse_temp)
        for k in range(depth // piece):
            span = pl.ds(stage * depth + k * piece, piece)
            logits = dot_nt(cents, toks_ref[span, :])
            lse = lses_ref[:, span]
            for r in range(0, tile, slice_rows):
                weights = jnp.exp(logits[r : r + slice_rows] - lse).astype(jnp.bfloat16)
                weights_ref[stage % 2, r : r + slice_rows, pl.ds(k * piece, piece)] = weights

    def gather_up(stage):
        toks = toks_ref[pl.ds(stage * depth, depth), :]
        rhs = jnp.concatenate([toks, jnp.ones_like(toks)], axis=1)
        part = jnp.dot(weights_ref[stage % 2], rhs, preferred_element_type=jnp.float32)
        if stage == 0:
            total_ref[...] = part
        else:
            total_ref[...] += part

    diagonal = lax.broadcasted_iota(jnp.int32, (128, 128), 0) == lax.broadcasted_iota(
        jnp.int32, (128, 128), 1
    )

    def run(r, waits=()):
        first = pl.multiple_of(r * tile, tile)
        for stage in range(stages):
            if waits:
                waits[stage].wait()
            weigh(first, stage)
            if stage:
                gather_up(stage - 1)
        gather_up(stages - 1)
        mass = total_ref[:, width : 2 * width]
        prior = prior_weight * cents_ref[pl.ds(first, tile), :].astype(jnp.float32)
        new = (total_ref[:, 0:width] + prior) / (mass + prior_weight)
        block = r // per_block
        coded = pl.multiple_of(first + block * (full - block_rows), 32)
        codes_ref[pl.ds(coded, tile), :] = encoded(new)
        for k in range(tile // 128):
            square = jnp.where(diagonal, mass[k * 128 : (k + 1) * 128, :], 0.0)
            mass_ref[r * (tile // 128) + k] = jnp.sum(square, axis=0, keepdims=True)

    loads[0].wait()
    loads[1].wait()
    run(0, loads[2:])
    if placing:
        placing.place()
    pl.loop(1, rows // tile)(run)

    for b in range(rows // block_rows):
        mass = mass_ref[b * block_rows // 128 : (b + 1) * block_rows // 128]
        mass = mass.reshape(block_rows // 128, 128)
        terms = split_exactly(mass)
        terms = jnp.concatenate([*terms, jnp.zeros_like(mass)], axis=0)
        codes_ref[b * full + block_rows : (b + 1) * full, :] = terms.astype(jnp.bfloat16)
    store = pltpu.make_async_copy(codes_ref, code_ref, sems.at[0])
    store.start()
    if placing:
        placing.finish()
    store.wait()


def updated_chunk(block, toks, lse, centroids, blocks, block_rows, after=(), received=None):
    all_count, width = toks.shape
    depth = divisor(all_count, 2048)
    tile = divisor(block_rows, 512)
    rows = blocks * block_rows
    full = coded_rows(block_rows)
    anywhere = pl.BlockSpec(memory_space=pl.ANY)
    place, operands = block.reshape(1), [toks, lse, centroids, *after]
    out_shape = [jax.ShapeDtypeStruct((blocks * full, width), jnp.bfloat16)]
    scratch_shapes = [
        pltpu.VMEM((all_count, width), jnp.bfloat16),
        pltpu.VMEM((1, all_count), jnp.float32),
        pltpu.VMEM((rows, width), jnp.bfloat16),
        pltpu.VMEM((blocks * full, width), jnp.bfloat16),
        pltpu.VMEM((2, tile, depth), jnp.bfloat16),
        pltpu.VMEM((tile, 2 * width), jnp.float32),
        pltpu.VMEM((rows // 128, 1, 128), jnp.float32),
        pltpu.SemaphoreType.DMA((2 + all_count // depth,)),
    ]
    aliases, pieces = {}, []
    if received:
        codes, starts, outs = received
        pieces = [len(parts) for parts in codes]
        place = jnp.concatenate([place, starts])
        operands += [*sum(codes, []), *outs]
        out_shape += [jax.ShapeDtypeStruct(out.shape, out.dtype) for out in outs]
        aliases = {len(operands) - 1: 1, len(operands): 2}
        scratch_shapes += Placing.scratch(len(codes), codes[0][0].shape[0] // full, block_rows, width)
    return pl.pallas_call(
        functools.partial(update_kernel, len(after), pieces, block_rows),
        grid_spec=pltpu.PrefetchScalarGridSpec(
            num_scalar_prefetch=1,
            grid=(1,),
            in_specs=[anywhere] * len(operands),
            out_specs=[anywhere] * len(out_shape),
            scratch_shapes=scratch_shapes,
        ),
        out_shape=out_shape,
        input_output_aliases=aliases,
        compiler_params=pltpu.CompilerParams(vmem_limit_bytes=vmem_bytes),
        cost_estimate=pl.CostEstimate(
            flops=6 * all_count * rows * width,
            bytes_accessed=(2 * all_count + 4 * rows) * width,
            transcendentals=all_count * rows,
        ),
        name="new_rows",
    )(place.astype(jnp.int32), *operands)


def place_kernel(chunks, block_rows, starts_ref, *refs):
    count = sum(map(sum, chunks))
    code_refs, outs, scratch = refs[:count], refs[count + 2 : count + 4], refs[count + 4 :]
    placings, first = [], 0
    for pieces in chunks:
        starts = starts_ref.at[pl.ds(first, len(pieces))]
        placings.append(
            Placing(block_rows, starts, pieces, code_refs[: sum(pieces)], outs, scratch[:4])
        )
        code_refs, scratch = code_refs[sum(pieces) :], scratch[4:]
        first += len(pieces)
    for placing in placings:
        placing.fetch()
    for placing in placings:
        placing.place()
    for placing in placings:
        placing.finish()


def placed(received, outs, block_rows):
    operands, starts, chunks, scratch_shapes = [], [], [], []
    for codes, start in received:
        chunks.append([len(parts) for parts in codes])
        operands += sum(codes, [])
        starts.append(start)
        rows, width = codes[0][0].shape
        blocks = rows // coded_rows(block_rows)
        scratch_shapes += Placing.scratch(len(codes), blocks, block_rows, width)
    anywhere = pl.BlockSpec(memory_space=pl.ANY)
    return pl.pallas_call(
        functools.partial(place_kernel, chunks, block_rows),
        grid_spec=pltpu.PrefetchScalarGridSpec(
            num_scalar_prefetch=1,
            grid=(1,),
            in_specs=[anywhere] * (len(operands) + 2),
            out_specs=[anywhere] * 2,
            scratch_shapes=scratch_shapes,
        ),
        out_shape=[jax.ShapeDtypeStruct(out.shape, out.dtype) for out in outs],
        input_output_aliases={1 + len(operands): 0, 2 + len(operands): 1},
        compiler_params=pltpu.CompilerParams(vmem_limit_bytes=vmem_bytes),
        name="placed_rows",
    )(jnp.concatenate(starts).astype(jnp.int32), *operands, *outs)


def combine_kernel(groups, parts_ref, out_ref):
    per_group = parts_ref.shape[0] // groups
    count = parts_ref.shape[2]
    for t in range(groups):
        parts = [parts_ref[t * per_group + k] for k in range(per_group)]
        top = functools.reduce(jnp.maximum, parts)
        total = functools.reduce(jnp.add, [jnp.exp(part - top) for part in parts])
        out_ref[:, t * count : (t + 1) * count] = top + jnp.log(total)


def combined_lse(parts, groups):
    return pl.pallas_call(
        functools.partial(combine_kernel, groups),
        out_shape=jax.ShapeDtypeStruct((1, groups * parts.shape[2]), jnp.float32),
        name="join_stats",
    )(parts)


def blank(shape):
    return pl.pallas_call(
        lambda out_ref: None,
        out_specs=pl.BlockSpec(memory_space=pl.ANY),
        out_shape=jax.ShapeDtypeStruct(shape, jnp.float32),
        name="blank",
    )()


def from_others(value, axis):
    size = lax.axis_size(axis)
    found = [value]
    for s in range(1, size):
        pairs = [(partner(k, s, size), k) for k in range(size)]
        found.append(lax.ppermute(value, axis, pairs))
    return found


def partner(me, s, size):
    return me ^ s if size & (size - 1) == 0 else (me - s) % size


def spread(codes):
    size = lax.axis_size("tok")
    if size != 4:
        return [[found] for found in from_others(codes, "tok")]

    def swap(part, mask):
        return lax.ppermute(part, "tok", [(k, k ^ mask) for k in range(4)])

    half = codes.shape[0] // 2
    one, two = swap(codes, 1), swap(codes, 2)
    return [[codes], [one], [two], [swap(one[:half], 2), swap(two[half:], 1)]]


def chunk_plan(blocks):
    plan = [1] if blocks > 1 else []
    blocks -= len(plan)
    while blocks:
        plan.insert(0, min(blocks, 2 if blocks > 3 else 3))
        blocks -= plan[0]
    return plan


def local(tokens, centroids):
    tok_size, cent_size = lax.axis_size("tok"), lax.axis_size("cent")
    me = lax.axis_index("tok")
    cent_count, width = centroids.shape
    share_rows = cent_count // tok_size

    toks = lax.all_gather(tokens, "tok", axis=0, tiled=True)
    own_lse = local_lse(tokens, centroids, tok_size * cent_size)
    parts = lax.all_to_all(own_lse, ("tok", "cent"), 0, 0, tiled=True)
    lse = combined_lse(parts, tok_size)

    block_rows = divisor(share_rows, 1024)
    sources = jnp.stack([partner(me, s, tok_size) for s in range(tok_size)])
    outs = blank((cent_count, width)), blank((cent_count // 128, 128))
    waiting, first = [], 0
    for blocks in chunk_plan(share_rows // block_rows):
        block = first * tok_size + me * blocks
        after = sum(waiting[-2][0][1:3], []) if len(waiting) > 1 else ()
        received = (*waiting.pop(0), outs) if len(waiting) == 3 else None
        codes, *placed_outs = updated_chunk(
            block, toks, lse, centroids, blocks, block_rows, after, received
        )
        outs = placed_outs or outs
        waiting.append((spread(codes), first * tok_size + sources * blocks))
        first += blocks
    if len(waiting) > 1:
        outs = placed(waiting[:-1], outs, block_rows)
    outs = placed(waiting[-1:], outs, block_rows)
    return outs[0], outs[1].reshape(cent_count)


def solution(mesh):
    placed_as = (P("tok", None), P("cent", None))
    return jax.shard_map(
        local, mesh=mesh, in_specs=placed_as, out_specs=(P("cent", None), P("cent")), check_vma=False
    )
```

profile of v0, /device:TPU:0, one launch (start us, length us, event | category | flops | bytes accessed | tf_op | source)
XLA Modules:
  0.0 216.0 jit_solution(10292816598287014128)
XLA Ops:
  7.2 0.7 all-gather.2.cloned.1.call-update
  7.9 49.3 %row_stats.1 = f32[32,1,2048]{2,1,0:T(1,128)} custom-call(bf16[2048,128]{1,0:T(8,128)(2,1)} %tok_ref.1, bf16[32768,128]{1,0:T(8,128)(2,1)} %refs_3_.7), custom_call_target="tpu_custom_call" | custom-call | flops 17179869184 | bytes 8912896 | tf_op jit(solution)/shard_map/row_stats/pallas_call | solution.py:121
  57.2 3.8 %all-to-all-start = ((f32[32,1,2048]{2,1,0:T(1,128)}), f32[32,1,2048]{2,1,0:T(1,128)S(1)}, u32[]{:S(2)}, u32[]{:S(2)}) async-start(f32[32,1,2048]{2,1,0:T(1,128)} %row_stats.1), calls=%async_computation | async-start | bytes 524288 | tf_op jit(solution)/shard_map/all_to_all | solution.py:501
  62.3 9.0 %all-to-all-done.parts_ref = f32[32,1,2048]{2,1,0:T(1,128)S(1)} async-done(((f32[32,1,2048]{2,1,0:T(1,128)}), f32[32,1,2048]{2,1,0:T(1,128)S(1)}, u32[]{:S(2)}, u32[]{:S(2)}) %all-to-all-start) | async-done | bytes 262176 | tf_op jit(solution)/shard_map/all_to_all | solution.py:501
  71.3 0.7 copy-done.6
  72.0 1.6 join_stats.1.refs_2_
  73.7 32.2 %new_rows.5.refs_6_ = bf16[3168,128]{1,0:T(8,128)(2,1)} custom-call(s32[1]{0:T(128)} %bitcast.6.refs_0_, bf16[8192,128]{1,0:T(8,128)(2,1)} %all-gather.2.cloned.1.call-done.refs_1_, f32[1,8192]{1,0:T(1,128)} %join_stats.1.refs_2_, bf16[32768,128]{1,0:T(8,128)(2,1)} %refs_3_.7), custom_call_target="tpu_custom_call" | custom-call | flops 19327352832 | bytes 3670016 | tf_op jit(solution)/shard_map/new_rows/pallas_call | solution.py:365
  106.4 0.8 collective-permute-start.3
  107.3 22.3 %new_rows.4.refs_0_ = bf16[2112,128]{1,0:T(8,128)(2,1)} custom-call(s32[1]{0:T(128)} %bitcast.5.refs_0_, bf16[8192,128]{1,0:T(8,128)(2,1)} %all-gather.2.cloned.1.call-done.refs_1_, f32[1,8192]{1,0:T(1,128)} %join_stats.1.refs_2_, bf16[32768,128]{1,0:T(8,128)(2,1)} %refs_3_.7), custom_call_target="tpu_custom_call" | custom-call | flops 12884901888 | bytes 3145728 | tf_op jit(solution)/shard_map/new_rows/pallas_call | solution.py:365
  129.6 1.3 collective-permute-start
  130.9 1.5 collective-permute-start.1
  133.1 0.9 collective-permute-start.5
  134.0 22.4 %new_rows.7.refs_5_ = bf16[2112,128]{1,0:T(8,128)(2,1)} custom-call(s32[1]{0:T(128)} %bitcast.7.refs_0_, bf16[8192,128]{1,0:T(8,128)(2,1)} %all-gather.2.cloned.1.call-done.refs_1_, f32[1,8192]{1,0:T(1,128)} %join_stats.1.refs_2_, bf16[32768,128]{1,0:T(8,128)(2,1)} %refs_3_.7, bf16[3168,128]{1,0:T(8,128)(2,1)} %copy-done.2, bf16[3168,128]{1,0:T(8,128)(2,1)} %copy-done.3), custom_call_target="tpu_custom_call" | custom-call | flops 12884901888 | bytes 3145728 | tf_op jit(solution)/shard_map/new_rows/pallas_call | solution.py:365
  156.3 1.3 collective-permute-start.12
  157.6 1.5 collective-permute-start.13
  159.2 0.8 copy-done.1
  160.1 0.7 copy-done.10
  160.8 16.4 %new_rows.6 = (bf16[1056,128]{1,0:T(8,128)(2,1)}, f32[32768,128]{1,0:T(8,128)}, f32[256,128]{1,0:T(8,128)}) custom-call(s32[5]{0:T(128)} %pad_add_fusion.1.refs_0_, bf16[8192,128]{1,0:T(8,128)(2,1)} %all-gather.2.cloned.1.call-done.refs_1_, f32[1,8192]{1,0:T(1,128)} %join_stats.1.refs_2_, ...), custom_call_target="tpu_custom_call", output_to_operand_aliasing={{1}: (11, {}), {2}: (12, {})} | custom-call | flops 6442450944 | bytes 2621440 | tf_op jit(solution)/shard_map/new_rows/pallas_call | solution.py:365
  177.2 0.9 collective-permute-start.6
  178.7 1.0 slice.36
  179.6 1.5 collective-permute-start.10
  181.2 1.0 slice.37
  182.2 1.3 collective-permute-start.11
  184.1 1.5 collective-permute-done.6.refs_1_
  185.6 1.2 collective-permute-start.15
  186.8 0.9 collective-permute-done.7.refs_2_
  188.3 5.2 %collective-permute-done.10.refs_3_ = bf16[1056,128]{1,0:T(8,128)(2,1)S(1)} collective-permute-done((bf16[1056,128]{1,0:T(8,128)(2,1)S(1)}, bf16[1056,128]{1,0:T(8,128)(2,1)S(1)}, u32[]{:S(2)}, u32[]{:S(2)}) %collective-permute-start.10) | collective-permute-done | bytes 270368 | tf_op jit(solution)/shard_map/ppermute | solution.py:477
  193.5 1.2 collective-permute-start.9
  195.4 2.4 %collective-permute-done.14.refs_8_ = bf16[1056,128]{1,0:T(8,128)(2,1)S(1)} collective-permute-done((bf16[1056,128]{1,0:T(8,128)(2,1)S(1)}, bf16[1056,128]{1,0:T(8,128)(2,1)S(1)}, u32[]{:S(2)}, u32[]{:S(2)}) %collective-permute-start.14) | collective-permute-done | bytes 270368 | tf_op jit(solution)/shard_map/ppermute | solution.py:477
  197.9 0.7 copy-done.13
  198.7 6.1 %placed_rows.2 = (f32[32768,128]{1,0:T(8,128)}, f32[256,128]{1,0:T(8,128)}) custom-call(s32[8]{0:T(128)} %pad_add_fusion.2.starts_ref, bf16[2112,128]{1,0:T(8,128)(2,1)} %new_rows.4.refs_0_, bf16[2112,128]{1,0:T(8,128)(2,1)} %copy-done, bf16[2112,128]{1,0:T(8,128)(2,1)} %copy-done.1, ...), custom_call_target="tpu_custom_call", output_to_operand_aliasing={{0}: (11, {}), {1}: (12, {})} | custom-call | tf_op jit(solution)/shard_map/placed_rows/pallas_call | solution.py:415
  205.6 3.3 %placed_rows.3 = (f32[32768,128]{1,0:T(8,128)}, f32[256,128]{1,0:T(8,128)}) custom-call(s32[4]{0:T(128)} %get-tuple-element.20.starts_ref, bf16[1056,128]{1,0:T(8,128)(2,1)} %get-tuple-element.9.refs_0_, bf16[1056,128]{1,0:T(8,128)(2,1)} %copy-done.7, bf16[1056,128]{1,0:T(8,128)(2,1)} %copy-done.8, ...), custom_call_target="tpu_custom_call", output_to_operand_aliasing={{0}: (6, {}), {1}: (7, {})} | custom-call | tf_op jit(solution)/shard_map/placed_rows/pallas_call | solution.py:415
  (61 shorter events, 5.9 us)
Async XLA Ops:
  7.2 66.5 %all-gather.2.cloned.1.call-start = ((), (), s32[]{:S(2)}) async-start(), calls=%async_computation.1 | async-start | bytes 2621440 | tf_op jit(solution)/shard_map/all_gather | solution.py:499
  57.2 14.2 %all-to-all-start = ((f32[32,1,2048]{2,1,0:T(1,128)}), f32[32,1,2048]{2,1,0:T(1,128)S(1)}, u32[]{:S(2)}, u32[]{:S(2)}) async-start(f32[32,1,2048]{2,1,0:T(1,128)} %row_stats.1), calls=%async_computation | async-start | bytes 524288 | tf_op jit(solution)/shard_map/all_to_all | solution.py:501
  105.9 26.6 %collective-permute-start.2 = (bf16[3168,128]{1,0:T(8,128)(2,1)}, bf16[3168,128]{1,0:T(8,128)(2,1)S(1)}, u32[]{:S(2)}, u32[]{:S(2)}) collective-permute-start(bf16[3168,128]{1,0:T(8,128)(2,1)} %new_rows.5.refs_6_), channel_id=1, source_target_pairs={{0,8},{8,0},{16,24},{24,16},{1,9},{9,1},{17,25},{25,17},{2,10},{10... | collective-permute-start | bytes 2433032 | tf_op jit(solution)/shard_map/ppermute | solution.py:477
  106.4 26.6 %collective-permute-start.3 = (bf16[3168,128]{1,0:T(8,128)(2,1)}, bf16[3168,128]{1,0:T(8,128)(2,1)S(1)}, u32[]{:S(2)}, u32[]{:S(2)}) collective-permute-start(bf16[3168,128]{1,0:T(8,128)(2,1)} %new_rows.5.refs_6_), channel_id=1, source_target_pairs={{0,16},{8,24},{16,0},{24,8},{1,17},{9,25},{17,1},{25,9},{2,18},{10... | collective-permute-start | bytes 2433032 | tf_op jit(solution)/shard_map/ppermute | solution.py:477
  129.6 28.0 %collective-permute-start = (bf16[2112,128]{1,0:T(8,128)(2,1)}, bf16[2112,128]{1,0:T(8,128)(2,1)S(1)}, u32[]{:S(2)}, u32[]{:S(2)}) collective-permute-start(bf16[2112,128]{1,0:T(8,128)(2,1)} %new_rows.4.refs_0_), channel_id=1, source_target_pairs={{0,8},{8,0},{16,24},{24,16},{1,9},{9,1},{17,25},{25,17},{2,10},{10... | collective-permute-start | bytes 1622024 | tf_op jit(solution)/shard_map/ppermute | solution.py:477
  130.9 28.2 %collective-permute-start.1 = (bf16[2112,128]{1,0:T(8,128)(2,1)}, bf16[2112,128]{1,0:T(8,128)(2,1)S(1)}, u32[]{:S(2)}, u32[]{:S(2)}) collective-permute-start(bf16[2112,128]{1,0:T(8,128)(2,1)} %new_rows.4.refs_0_), channel_id=1, source_target_pairs={{0,16},{8,24},{16,0},{24,8},{1,17},{9,25},{17,1},{25,9},{2,18},{10... | collective-permute-start | bytes 1622024 | tf_op jit(solution)/shard_map/ppermute | solution.py:477
  132.4 1.5 copy-start.2
  132.5 26.7 %collective-permute-start.4 = (bf16[1584,128]{1,0:T(8,128)(2,1)S(1)}, bf16[1584,128]{1,0:T(8,128)(2,1)S(1)}, u32[]{:S(2)}, u32[]{:S(2)}) collective-permute-start(bf16[1584,128]{1,0:T(8,128)(2,1)S(1)} %slice.32), channel_id=1, source_target_pairs={{0,16},{8,24},{16,0},{24,8},{1,17},{9,25},{17,1},{25,9},{2,18},{10... | collective-permute-start | bytes 1216520 | tf_op jit(solution)/shard_map/ppermute | solution.py:477
  133.1 0.9 copy-start.3
  133.1 26.1 %collective-permute-start.5 = (bf16[1584,128]{1,0:T(8,128)(2,1)S(1)}, bf16[1584,128]{1,0:T(8,128)(2,1)S(1)}, u32[]{:S(2)}, u32[]{:S(2)}) collective-permute-start(bf16[1584,128]{1,0:T(8,128)(2,1)S(1)} %slice.33), channel_id=1, source_target_pairs={{0,8},{8,0},{16,24},{24,16},{1,9},{9,1},{17,25},{25,17},{2,10},{10... | collective-permute-start | bytes 1216520 | tf_op jit(solution)/shard_map/ppermute | solution.py:477
  156.3 25.8 %collective-permute-start.12 = (bf16[2112,128]{1,0:T(8,128)(2,1)}, bf16[2112,128]{1,0:T(8,128)(2,1)S(1)}, u32[]{:S(2)}, u32[]{:S(2)}) collective-permute-start(bf16[2112,128]{1,0:T(8,128)(2,1)} %new_rows.7.refs_5_), channel_id=1, source_target_pairs={{0,8},{8,0},{16,24},{24,16},{1,9},{9,1},{17,25},{25,17},{2,10},{10... | collective-permute-start | bytes 1622024 | tf_op jit(solution)/shard_map/ppermute | solution.py:477
  157.6 1.5 copy-start
  157.6 25.9 %collective-permute-start.13 = (bf16[2112,128]{1,0:T(8,128)(2,1)}, bf16[2112,128]{1,0:T(8,128)(2,1)S(1)}, u32[]{:S(2)}, u32[]{:S(2)}) collective-permute-start(bf16[2112,128]{1,0:T(8,128)(2,1)} %new_rows.7.refs_5_), channel_id=1, source_target_pairs={{0,16},{8,24},{16,0},{24,8},{1,17},{9,25},{17,1},{25,9},{2,18},{10... | collective-permute-start | bytes 1622024 | tf_op jit(solution)/shard_map/ppermute | solution.py:477
  159.2 0.8 copy-start.1
  159.2 0.9 copy-start.9
  160.1 0.8 copy-start.10
  177.2 8.4 %collective-permute-start.6 = (bf16[1056,128]{1,0:T(8,128)(2,1)}, bf16[1056,128]{1,0:T(8,128)(2,1)S(1)}, u32[]{:S(2)}, u32[]{:S(2)}) collective-permute-start(bf16[1056,128]{1,0:T(8,128)(2,1)} %get-tuple-element.9.refs_0_), channel_id=1, source_target_pairs={{0,8},{8,0},{16,24},{24,16},{1,9},{9,1},{17,25},{25,17},{2,10},{10... | collective-permute-start | bytes 811016 | tf_op jit(solution)/shard_map/ppermute | solution.py:477
  178.1 9.6 %collective-permute-start.7 = (bf16[1056,128]{1,0:T(8,128)(2,1)}, bf16[1056,128]{1,0:T(8,128)(2,1)S(1)}, u32[]{:S(2)}, u32[]{:S(2)}) collective-permute-start(bf16[1056,128]{1,0:T(8,128)(2,1)} %get-tuple-element.9.refs_0_), channel_id=1, source_target_pairs={{0,16},{8,24},{16,0},{24,8},{1,17},{9,25},{17,1},{25,9},{2,18},{10... | collective-permute-start | bytes 811016 | tf_op jit(solution)/shard_map/ppermute | solution.py:477
  179.6 13.9 %collective-permute-start.10 = (bf16[1056,128]{1,0:T(8,128)(2,1)S(1)}, bf16[1056,128]{1,0:T(8,128)(2,1)S(1)}, u32[]{:S(2)}, u32[]{:S(2)}) collective-permute-start(bf16[1056,128]{1,0:T(8,128)(2,1)S(1)} %slice.36), channel_id=1, source_target_pairs={{0,16},{8,24},{16,0},{24,8},{1,17},{9,25},{17,1},{25,9},{2,18},{10... | collective-permute-start | bytes 811016 | tf_op jit(solution)/shard_map/ppermute | solution.py:477
  182.2 15.7 %copy-start.4 = (bf16[2112,128]{1,0:T(8,128)(2,1)}, bf16[2112,128]{1,0:T(8,128)(2,1)S(1)}, u32[]{:S(2)}) copy-start(bf16[2112,128]{1,0:T(8,128)(2,1)S(1)} %collective-permute-done.12.refs_6_) | copy-start | bytes 1622020
  182.2 13.2 %collective-permute-start.11 = (bf16[1056,128]{1,0:T(8,128)(2,1)S(1)}, bf16[1056,128]{1,0:T(8,128)(2,1)S(1)}, u32[]{:S(2)}, u32[]{:S(2)}) collective-permute-start(bf16[1056,128]{1,0:T(8,128)(2,1)S(1)} %slice.37), channel_id=1, source_target_pairs={{0,8},{8,0},{16,24},{24,16},{1,9},{9,1},{17,25},{25,17},{2,10},{10... | collective-permute-start | bytes 811016 | tf_op jit(solution)/shard_map/ppermute | solution.py:477
  183.5 14.4 %copy-start.5 = (bf16[2112,128]{1,0:T(8,128)(2,1)}, bf16[2112,128]{1,0:T(8,128)(2,1)S(1)}, u32[]{:S(2)}) copy-start(bf16[2112,128]{1,0:T(8,128)(2,1)S(1)} %collective-permute-done.13.refs_7_) | copy-start | bytes 1622020
  183.5 14.4 %collective-permute-start.14 = (bf16[1056,128]{1,0:T(8,128)(2,1)S(1)}, bf16[1056,128]{1,0:T(8,128)(2,1)S(1)}, u32[]{:S(2)}, u32[]{:S(2)}) collective-permute-start(bf16[1056,128]{1,0:T(8,128)(2,1)S(1)} %slice.38), channel_id=1, source_target_pairs={{0,16},{8,24},{16,0},{24,8},{1,17},{9,25},{17,1},{25,9},{2,18},{10... | collective-permute-start | bytes 811016 | tf_op jit(solution)/shard_map/ppermute | solution.py:477
  185.6 19.3 %copy-start.7 = (bf16[1056,128]{1,0:T(8,128)(2,1)}, bf16[1056,128]{1,0:T(8,128)(2,1)S(1)}, u32[]{:S(2)}) copy-start(bf16[1056,128]{1,0:T(8,128)(2,1)S(1)} %collective-permute-done.6.refs_1_) | copy-start | bytes 811012
  185.6 12.2 %collective-permute-start.15 = (bf16[1056,128]{1,0:T(8,128)(2,1)S(1)}, bf16[1056,128]{1,0:T(8,128)(2,1)S(1)}, u32[]{:S(2)}, u32[]{:S(2)}) collective-permute-start(bf16[1056,128]{1,0:T(8,128)(2,1)S(1)} %slice.39), channel_id=1, source_target_pairs={{0,8},{8,0},{16,24},{24,16},{1,9},{9,1},{17,25},{25,17},{2,10},{10... | collective-permute-start | bytes 811016 | tf_op jit(solution)/shard_map/ppermute | solution.py:477
  187.7 17.2 %copy-start.8 = (bf16[1056,128]{1,0:T(8,128)(2,1)}, bf16[1056,128]{1,0:T(8,128)(2,1)S(1)}, u32[]{:S(2)}) copy-start(bf16[1056,128]{1,0:T(8,128)(2,1)S(1)} %collective-permute-done.7.refs_2_) | copy-start | bytes 811012
  187.7 17.1 %collective-permute-start.8 = (bf16[528,128]{1,0:T(8,128)(2,1)S(1)}, bf16[528,128]{1,0:T(8,128)(2,1)S(1)}, u32[]{:S(2)}, u32[]{:S(2)}) collective-permute-start(bf16[528,128]{1,0:T(8,128)(2,1)S(1)} %slice.34), channel_id=1, source_target_pairs={{0,16},{8,24},{16,0},{24,8},{1,17},{9,25},{17,1},{25,9},{2,18},{10... | collective-permute-start | bytes 405512 | tf_op jit(solution)/shard_map/ppermute | solution.py:477
  193.5 4.4 %copy-start.11 = (bf16[1056,128]{1,0:T(8,128)(2,1)}, bf16[1056,128]{1,0:T(8,128)(2,1)S(1)}, u32[]{:S(2)}) copy-start(bf16[1056,128]{1,0:T(8,128)(2,1)S(1)} %collective-permute-done.10.refs_3_) | copy-start | bytes 811012
  193.5 11.3 %collective-permute-start.9 = (bf16[528,128]{1,0:T(8,128)(2,1)S(1)}, bf16[528,128]{1,0:T(8,128)(2,1)S(1)}, u32[]{:S(2)}, u32[]{:S(2)}) collective-permute-start(bf16[528,128]{1,0:T(8,128)(2,1)S(1)} %slice.35), channel_id=1, source_target_pairs={{0,8},{8,0},{16,24},{24,16},{1,9},{9,1},{17,25},{25,17},{2,10},{10... | collective-permute-start | bytes 405512 | tf_op jit(solution)/shard_map/ppermute | solution.py:477
  195.4 2.5 %copy-start.12 = (bf16[1056,128]{1,0:T(8,128)(2,1)}, bf16[1056,128]{1,0:T(8,128)(2,1)S(1)}, u32[]{:S(2)}) copy-start(bf16[1056,128]{1,0:T(8,128)(2,1)S(1)} %collective-permute-done.11.refs_4_) | copy-start | bytes 811012
  197.9 0.7 copy-start.13
  197.9 0.8 copy-start.14
  (3 other events, 2.1 us)
Sparse Core Ops, SparseCore 0:
  9.8 38.0 all-gather.1
where the time goes:
time: 219 us; the launch traced here: 216 us
  Pallas kernels  154 us (70%)
  starting transfers between devices  20.1 us (9%)
  waiting for transfers between devices  19.9 us (9%)
  between operations  14.6 us (7%)
  local copies, waits for them, and re-layouts  5.88 us (3%)
    pallas_call x4, Pallas kernels, updated_chunk(): pl.pallas_call(functools.partial(update_kernel, len(after), pieces, block...  93.3 us
    pallas_call x1, Pallas kernels, local_lse(): pl.pallas_call(functools.partial(stats_kernel, sub_rows, tok_cols), grid=...  49.3 us
    ppermute x16, starting transfers between devices, swap(): return lax.ppermute(part, 'tok', [(k, k ^ mask) for k in range(4)])  16.2 us
    ppermute x16, waiting for transfers between devices, swap(): return lax.ppermute(part, 'tok', [(k, k ^ mask) for k in range(4)])  10.1 us
    pallas_call x2, Pallas kernels, placed(): pl.pallas_call(functools.partial(place_kernel, chunks, block_rows), grid_...  9.48 us
    all_to_all x1, waiting for transfers between devices, local(): parts = lax.all_to_all(own_lse, ('tok', 'cent'), 0, 0, tiled=True)  9.03 us
  transfers between devices with their start and end apart: 18, of which 5 were waited for; matrix products, arithmetic and copies ran while one was open for 2% of the time, Pallas kernels for 55%

commit v1 on v0

--- a/solution.py
+++ b/solution.py
@@ -33,6 +33,12 @@
         half = len(parts) // 2
         parts = [combine(parts[2 * k], parts[2 * k + 1]) for k in range(half)] + parts[2 * half :]
     return parts[0]
+
+
+def split_exactly(x):
+    high = x.astype(jnp.bfloat16).astype(jnp.float32)
+    middle = (x - high).astype(jnp.bfloat16).astype(jnp.float32)
+    return high, middle, x - high - middle
 
 
 def stats_kernel(
@@ -51,15 +57,26 @@
     def dot(a, b):
         return jnp.dot(a, b, preferred_element_type=jnp.float32)
 
+    width = tok_ref.shape[1]
+
     @pl.when(step == 0)
     def _():
         @pl.loop(0, col_blocks)
         def _(t):
             flipped = (tok_ref[columns(t), :] * jnp.bfloat16(inverse_temp)).T
-            flip_ref[:, columns(t)] = flipped
+            flip_ref[0:width, columns(t)] = flipped
             logits = dot(cent_ref[0:128, :], flipped)
             top = jnp.max(fold_rows(logits, jnp.maximum), axis=0, keepdims=True)
-            base_ref[:, columns(t)] = top + headroom
+            base = top + headroom
+            base_ref[:, columns(t)] = base
+            row = lax.broadcasted_iota(jnp.int32, (width, tok_cols), 0)
+            terms = jnp.zeros((width, tok_cols), jnp.float32)
+            for k, term in enumerate(split_exactly(-base)):
+                terms = jnp.where(row == k, term, terms)
+            flip_ref[width:, columns(t)] = terms.astype(jnp.bfloat16)
+
+    lane = lax.broadcasted_iota(jnp.int32, (sub_rows, width), 1)
+    ones = jnp.where(lane < 3, 1.0, 0.0).astype(jnp.bfloat16)
 
     @pl.loop(0, col_blocks)
     def _(t):
@@ -67,9 +84,10 @@
         shift = base_ref[:, columns(t)]
         for sub in range(subs):
             total = jnp.zeros((8, tok_cols), jnp.float32)
-            logits = dot(cent_ref[pl.ds(sub * sub_rows, sub_rows), :], rhs)
+            lhs = jnp.concatenate([cent_ref[pl.ds(sub * sub_rows, sub_rows), :], ones], axis=1)
+            logits = dot(lhs, rhs)
             for first in range(0, sub_rows, slice_rows):
-                scaled = jnp.exp(logits[first : first + slice_rows] - shift)
+                scaled = jnp.exp(logits[first : first + slice_rows])
                 total = total + fold_rows(scaled, jnp.add)
             sums_ref[step * subs + sub, :, columns(t)] = total
             shift_ref[step * subs + sub, :, columns(t)] = shift
@@ -89,7 +107,8 @@
             def _():
                 sub, t = k // redo_blocks, lax.rem(k, redo_blocks)
                 first = pl.multiple_of(sub * sub_rows, sub_rows)
-                logits = dot(cent_ref[pl.ds(first, sub_rows), :], flip_ref[:, columns(t, redo_cols)])
+                rhs = flip_ref[0:width, columns(t, redo_cols)]
+                logits = dot(cent_ref[pl.ds(first, sub_rows), :], rhs)
                 top = jnp.max(fold_rows(logits, jnp.maximum), axis=0, keepdims=True)
                 total = fold_rows(jnp.exp(logits - top), jnp.add)
                 sums_ref[step * subs + sub, :, columns(t, redo_cols)] = total
@@ -128,7 +147,7 @@
         out_specs=pl.BlockSpec((copies, 1, tok_count), lambda j: (0, 0, 0)),
         out_shape=jax.ShapeDtypeStruct((copies, 1, tok_count), jnp.float32),
         scratch_shapes=[
-            pltpu.VMEM((width, tok_count), jnp.bfloat16),
+            pltpu.VMEM((2 * width, tok_count), jnp.bfloat16),
             pltpu.VMEM((1, tok_count), jnp.float32),
             pltpu.VMEM((subs, 1, tok_count), jnp.float32),
             pltpu.VMEM((subs, 8, tok_count), jnp.float32),
@@ -155,12 +174,6 @@
     return jnp.where(code < 0, -size, jnp.where(code > 0, size, 0.0))
 
 
-def split_exactly(x):
-    high = x.astype(jnp.bfloat16).astype(jnp.float32)
-    middle = (x - high).astype(jnp.bfloat16).astype(jnp.float32)
-    return high, middle, x - high - middle
-
-
 class Placing:
     def __init__(self, block_rows, starts_ref, pieces, code_refs, outs, scratch):
         self.block_rows, self.starts_ref = block_rows, starts_ref
@@ -247,43 +260,33 @@
         scratch = refs[5:]
         starts_ref = place_ref.at[pl.ds(1, len(pieces))]
         placing = Placing(
-            block_rows, starts_ref, pieces, code_refs, (updated_ref, masses_ref), scratch[8:]
+            block_rows, starts_ref, pieces, code_refs, (updated_ref, masses_ref), scratch[3:]
         )
     else:
         code_ref, scratch, placing = refs[0], refs[1:], None
-    toks_ref, lses_ref, cents_ref, codes_ref, weights_ref, total_ref, mass_ref, sems = scratch[:8]
-    rows, width = cents_ref.shape
+    weights_ref, total_ref, mass_ref = scratch[:3]
+    step, steps = pl.program_id(0), pl.num_programs(0)
+    width = tok_ref.shape[1]
     _, tile, depth = weights_ref.shape
     piece = divisor(depth, 512)
-    stages = toks_ref.shape[0] // depth
-    full = coded_rows(block_rows)
-    per_block = block_rows // tile
-
-    first_row = pl.multiple_of(place_ref[0] * block_rows, block_rows)
-    loads = [
-        pltpu.make_async_copy(cent_ref.at[pl.ds(first_row, rows), :], cents_ref, sems.at[0]),
-        pltpu.make_async_copy(lse_ref, lses_ref, sems.at[1]),
-    ]
-    for stage in range(stages):
-        span = pl.ds(stage * depth, depth)
-        loads.append(pltpu.make_async_copy(tok_ref.at[span, :], toks_ref.at[span, :], sems.at[2 + stage]))
-    for load in loads:
-        load.start()
+    stages = tok_ref.shape[0] // depth
+    tiles = block_rows // tile
+
     if placing:
-        placing.fetch()
+        pl.when(step == 0)(placing.fetch)
 
     def weigh(first, stage):
-        cents = cents_ref[pl.ds(first, tile), :] * jnp.bfloat16(inverse_temp)
+        cents = cent_ref[pl.ds(first, tile), :] * jnp.bfloat16(inverse_temp)
         for k in range(depth // piece):
             span = pl.ds(stage * depth + k * piece, piece)
-            logits = dot_nt(cents, toks_ref[span, :])
-            lse = lses_ref[:, span]
+            logits = dot_nt(cents, tok_ref[span, :])
+            lse = lse_ref[:, span]
             for r in range(0, tile, slice_rows):
                 weights = jnp.exp(logits[r : r + slice_rows] - lse).astype(jnp.bfloat16)
                 weights_ref[stage % 2, r : r + slice_rows, pl.ds(k * piece, piece)] = weights
 
     def gather_up(stage):
-        toks = toks_ref[pl.ds(stage * depth, depth), :]
+        toks = tok_ref[pl.ds(stage * depth, depth), :]
         rhs = jnp.concatenate([toks, jnp.ones_like(toks)], axis=1)
         part = jnp.dot(weights_ref[stage % 2], rhs, preferred_element_type=jnp.float32)
         if stage == 0:
@@ -295,43 +298,31 @@
         jnp.int32, (128, 128), 1
     )
 
-    def run(r, waits=()):
+    def run(r):
         first = pl.multiple_of(r * tile, tile)
-        for stage in range(stages):
-            if waits:
-                waits[stage].wait()
+        weigh(first, 0)
+        for stage in range(1, stages):
             weigh(first, stage)
-            if stage:
-                gather_up(stage - 1)
+            gather_up(stage - 1)
         gather_up(stages - 1)
         mass = total_ref[:, width : 2 * width]
-        prior = prior_weight * cents_ref[pl.ds(first, tile), :].astype(jnp.float32)
+        prior = prior_weight * cent_ref[pl.ds(first, tile), :].astype(jnp.float32)
         new = (total_ref[:, 0:width] + prior) / (mass + prior_weight)
-        block = r // per_block
-        coded = pl.multiple_of(first + block * (full - block_rows), 32)
-        codes_ref[pl.ds(coded, tile), :] = encoded(new)
+        code_ref[pl.ds(first, tile), :] = encoded(new)
         for k in range(tile // 128):
             square = jnp.where(diagonal, mass[k * 128 : (k + 1) * 128, :], 0.0)
-            mass_ref[r * (tile // 128) + k] = jnp.sum(square, axis=0, keepdims=True)
-
-    loads[0].wait()
-    loads[1].wait()
-    run(0, loads[2:])
+            mass_ref[pl.ds(r * (tile // 128) + k, 1), :] = jnp.sum(square, axis=0, keepdims=True)
+
+    pl.loop(0, tiles // 2)(run)
     if placing:
-        placing.place()
-    pl.loop(1, rows // tile)(run)
-
-    for b in range(rows // block_rows):
-        mass = mass_ref[b * block_rows // 128 : (b + 1) * block_rows // 128]
-        mass = mass.reshape(block_rows // 128, 128)
-        terms = split_exactly(mass)
-        terms = jnp.concatenate([*terms, jnp.zeros_like(mass)], axis=0)
-        codes_ref[b * full + block_rows : (b + 1) * full, :] = terms.astype(jnp.bfloat16)
-    store = pltpu.make_async_copy(codes_ref, code_ref, sems.at[0])
-    store.start()
+        pl.when(step == 0)(placing.place)
+    pl.loop(tiles // 2, tiles)(run)
+
+    terms = split_exactly(mass_ref[...])
+    terms = jnp.concatenate([*terms, jnp.zeros_like(terms[0])], axis=0)
+    code_ref[block_rows : block_rows + terms.shape[0], :] = terms.astype(jnp.bfloat16)
     if placing:
-        placing.finish()
-    store.wait()
+        pl.when(step == steps - 1)(placing.finish)
 
 
 def updated_chunk(block, toks, lse, centroids, blocks, block_rows, after=(), received=None):
@@ -341,17 +332,19 @@
     rows = blocks * block_rows
     full = coded_rows(block_rows)
     anywhere = pl.BlockSpec(memory_space=pl.ANY)
+    whole = lambda j, place: (0, 0)
     place, operands = block.reshape(1), [toks, lse, centroids, *after]
+    in_specs = [
+        pl.BlockSpec((all_count, width), whole),
+        pl.BlockSpec((1, all_count), whole),
+        pl.BlockSpec((block_rows, width), lambda j, place: (place[0] + j, 0)),
+    ] + [anywhere] * len(after)
+    out_specs = [pl.BlockSpec((full, width), lambda j, place: (j, 0))]
     out_shape = [jax.ShapeDtypeStruct((blocks * full, width), jnp.bfloat16)]
     scratch_shapes = [
-        pltpu.VMEM((all_count, width), jnp.bfloat16),
-        pltpu.VMEM((1, all_count), jnp.float32),
-        pltpu.VMEM((rows, width), jnp.bfloat16),
-        pltpu.VMEM((blocks * full, width), jnp.bfloat16),
         pltpu.VMEM((2, tile, depth), jnp.bfloat16),
         pltpu.VMEM((tile, 2 * width), jnp.float32),
-        pltpu.VMEM((rows // 128, 1, 128), jnp.float32),
-        pltpu.SemaphoreType.DMA((2 + all_count // depth,)),
+        pltpu.VMEM((block_rows // 128, 128), jnp.float32),
     ]
     aliases, pieces = {}, []
     if received:
@@ -359,6 +352,8 @@
         pieces = [len(parts) for parts in codes]
         place = jnp.concatenate([place, starts])
         operands += [*sum(codes, []), *outs]
+        in_specs += [anywhere] * (sum(pieces) + 2)
+        out_specs += [anywhere] * 2
         out_shape += [jax.ShapeDtypeStruct(out.shape, out.dtype) for out in outs]
         aliases = {len(operands) - 1: 1, len(operands): 2}
         scratch_shapes += Placing.scratch(len(codes), codes[0][0].shape[0] // full, block_rows, width)
@@ -366,9 +361,9 @@
         functools.partial(update_kernel, len(after), pieces, block_rows),
         grid_spec=pltpu.PrefetchScalarGridSpec(
             num_scalar_prefetch=1,
-            grid=(1,),
-            in_specs=[anywhere] * len(operands),
-            out_specs=[anywhere] * len(out_shape),
+            grid=(blocks,),
+            in_specs=in_specs,
+            out_specs=out_specs,
             scratch_shapes=scratch_shapes,
         ),
         out_shape=out_shape,
@@ -468,26 +463,12 @@
     return me ^ s if size & (size - 1) == 0 else (me - s) % size
 
 
-def spread(codes):
-    size = lax.axis_size("tok")
-    if size != 4:
-        return [[found] for found in from_others(codes, "tok")]
-
-    def swap(part, mask):
-        return lax.ppermute(part, "tok", [(k, k ^ mask) for k in range(4)])
-
-    half = codes.shape[0] // 2
-    one, two = swap(codes, 1), swap(codes, 2)
-    return [[codes], [one], [two], [swap(one[:half], 2), swap(two[half:], 1)]]
-
-
 def chunk_plan(blocks):
-    plan = [1] if blocks > 1 else []
-    blocks -= len(plan)
-    while blocks:
-        plan.insert(0, min(blocks, 2 if blocks > 3 else 3))
-        blocks -= plan[0]
-    return plan
+    plan = []
+    while blocks > 2:
+        plan.append(2)
+        blocks -= 2
+    return plan + [1] * blocks
 
 
 def local(tokens, centroids):
@@ -505,15 +486,21 @@
     sources = jnp.stack([partner(me, s, tok_size) for s in range(tok_size)])
     outs = blank((cent_count, width)), blank((cent_count // 128, 128))
     waiting, first = [], 0
-    for blocks in chunk_plan(share_rows // block_rows):
+    plan = chunk_plan(share_rows // block_rows)
+    for k, blocks in enumerate(plan):
         block = first * tok_size + me * blocks
-        after = sum(waiting[-2][0][1:3], []) if len(waiting) > 1 else ()
-        received = (*waiting.pop(0), outs) if len(waiting) == 3 else None
+        after, received = (), None
+        if len(waiting) == 2:
+            if k + 1 < len(plan):
+                received = (*waiting.pop(0), outs)
+            else:
+                after = sum(waiting[0][0][1:], [])
         codes, *placed_outs = updated_chunk(
             block, toks, lse, centroids, blocks, block_rows, after, received
         )
         outs = placed_outs or outs
-        waiting.append((spread(codes), first * tok_size + sources * blocks))
+        found = [[part] for part in from_others(codes, "tok")]
+        waiting.append((found, first * tok_size + sources * blocks))
         first += blocks
     if len(waiting) > 1:
         outs = placed(waiting[:-1], outs, block_rows)

time: 219 us -> 224 us (1.023)
  Pallas kernels: 154 us -> 162 us
  waiting for transfers between devices: 19.9 us -> 14.5 us
    pallas_call x4 -> x5, Pallas kernels: 93.3 us -> 102 us  [updated_chunk(): pl.pallas_call(functools.partial(update_kernel, len(after), pieces, block...]
    ppermute x16 -> x15, waiting for transfers between devices: 10.1 us -> 5.26 us  [from_others(): found.append(lax.ppermute(value, axis, pairs))]
    unnamed x34 -> x32, local copies, waits for them, and re-layouts: 3.83 us -> 5.62 us
    ppermute x16 -> x15, starting transfers between devices: 16.2 us -> 17.6 us  [from_others(): found.append(lax.ppermute(value, axis, pairs))]
  transfers between devices with their start and end apart: 18 -> 17, of which waited for: 5 -> 4; matrix products, arithmetic and copies ran while one was open for 2% -> 1% of each run, Pallas kernels for 55% -> 63%
where the time goes in v1:
time: 224 us; the launch traced here: 221 us
  Pallas kernels  162 us (72%)
  starting transfers between devices  21.5 us (10%)
  between operations  14.7 us (7%)
  waiting for transfers between devices  14.5 us (6%)
  local copies, waits for them, and re-layouts  5.62 us (3%)
  other arithmetic  2.41 us (1%)
    pallas_call x5, Pallas kernels, updated_chunk(): pl.pallas_call(functools.partial(update_kernel, len(after), pieces, block...  102 us
    pallas_call x1, Pallas kernels, local_lse(): pl.pallas_call(functools.partial(stats_kernel, sub_rows, tok_cols), grid=...  49.5 us
    ppermute x15, starting transfers between devices, from_others(): found.append(lax.ppermute(value, axis, pairs))  17.6 us
    pallas_call x2, Pallas kernels, placed(): pl.pallas_call(functools.partial(place_kernel, chunks, block_rows), grid_...  8.54 us
    all_to_all x1, waiting for transfers between devices, local(): parts = lax.all_to_all(own_lse, ('tok', 'cent'), 0, 0, tiled=True)  8.53 us
    unnamed x32, local copies, waits for them, and re-layouts  5.62 us
    ppermute x15, waiting for transfers between devices, from_others(): found.append(lax.ppermute(value, axis, pairs))  5.26 us
  transfers between devices with their start and end apart: 17, of which 4 were waited for; matrix products, arithmetic and copies ran while one was open for 1% of the time, Pallas kernels for 63%

profile of v1, /device:TPU:0, one launch (start us, length us, event | category | flops | bytes accessed | tf_op | source)
XLA Modules:
  0.0 220.8 jit_solution(2148055276730367292)
XLA Ops:
  7.2 0.7 all-gather.2.cloned.1.call-update
  7.9 49.5 %row_stats.1 = f32[32,1,2048]{2,1,0:T(1,128)} custom-call(bf16[2048,128]{1,0:T(8,128)(2,1)} %tok_ref.1, bf16[32768,128]{1,0:T(8,128)(2,1)} %refs_3_.9), custom_call_target="tpu_custom_call" | custom-call | flops 17179869184 | bytes 8912896 | tf_op jit(solution)/shard_map/row_stats/pallas_call | solution.py:140
  57.4 3.9 %all-to-all-start = ((f32[32,1,2048]{2,1,0:T(1,128)}), f32[32,1,2048]{2,1,0:T(1,128)S(1)}, u32[]{:S(2)}, u32[]{:S(2)}) async-start(f32[32,1,2048]{2,1,0:T(1,128)} %row_stats.1), calls=%async_computation | async-start | bytes 524288 | tf_op jit(solution)/shard_map/all_to_all | solution.py:482
  63.1 8.5 %all-to-all-done.parts_ref = f32[32,1,2048]{2,1,0:T(1,128)S(1)} async-done(((f32[32,1,2048]{2,1,0:T(1,128)}), f32[32,1,2048]{2,1,0:T(1,128)S(1)}, u32[]{:S(2)}, u32[]{:S(2)}) %all-to-all-start) | async-done | bytes 262176 | tf_op jit(solution)/shard_map/all_to_all | solution.py:482
  71.6 0.7 copy-done
  72.3 1.6 join_stats.1.refs_2_
  74.0 20.5 %new_rows.5.refs_4_ = bf16[2112,128]{1,0:T(8,128)(2,1)} custom-call(s32[1]{0:T(128)} %bitcast.6.refs_0_, bf16[8192,128]{1,0:T(8,128)(2,1)} %all-gather.2.cloned.1.call-done.refs_1_, f32[1,8192]{1,0:T(1,128)} %join_stats.1.refs_2_, bf16[32768,128]{1,0:T(8,128)(2,1)} %refs_3_.9), custom_call_target="tpu_custom_call" | custom-call | flops 12884901888 | bytes 3145728 | tf_op jit(solution)/shard_map/new_rows/pallas_call | solution.py:360
  95.0 0.8 collective-permute-start.1
  95.9 2.2 collective-permute-start.2
  98.0 20.9 %new_rows.8.refs_4_ = bf16[2112,128]{1,0:T(8,128)(2,1)} custom-call(s32[1]{0:T(128)} %bitcast.8.refs_0_, bf16[8192,128]{1,0:T(8,128)(2,1)} %all-gather.2.cloned.1.call-done.refs_1_, f32[1,8192]{1,0:T(1,128)} %join_stats.1.refs_2_, bf16[32768,128]{1,0:T(8,128)(2,1)} %refs_3_.9), custom_call_target="tpu_custom_call" | custom-call | flops 12884901888 | bytes 3145728 | tf_op jit(solution)/shard_map/new_rows/pallas_call | solution.py:360
  119.4 1.4 collective-permute-start.11
  120.9 1.5 collective-permute-start.9
  122.4 0.8 copy-done.14
  123.2 0.8 copy-done.15
  124.0 35.1 %new_rows.6 = (bf16[2112,128]{1,0:T(8,128)(2,1)}, f32[32768,128]{1,0:T(8,128)}, f32[256,128]{1,0:T(8,128)}) custom-call(s32[5]{0:T(128)} %pad_add_fusion.1.refs_0_, bf16[8192,128]{1,0:T(8,128)(2,1)} %all-gather.2.cloned.1.call-done.refs_1_, f32[1,8192]{1,0:T(1,128)} %join_stats.1.refs_2_, ...), custom_call_target="tpu_custom_call", output_to_operand_aliasing={{1}: (8, {}), {2}: (9, {})} | custom-call | flops 12884901888 | bytes 3145728 | tf_op jit(solution)/shard_map/new_rows/pallas_call | solution.py:360
  159.1 0.8 collective-permute-start.3
  159.9 0.6 collective-permute-start.4
  160.5 2.2 collective-permute-start.5
  162.7 0.8 copy-done.5
  163.7 14.3 %new_rows.9 = (bf16[1056,128]{1,0:T(8,128)(2,1)}, f32[32768,128]{1,0:T(8,128)}, f32[256,128]{1,0:T(8,128)}) custom-call(s32[5]{0:T(128)} %pad_add_fusion.3.refs_0_, bf16[8192,128]{1,0:T(8,128)(2,1)} %all-gather.2.cloned.1.call-done.refs_1_, f32[1,8192]{1,0:T(1,128)} %join_stats.1.refs_2_, ...), custom_call_target="tpu_custom_call", output_to_operand_aliasing={{1}: (8, {}), {2}: (9, {})} | custom-call | flops 6442450944 | bytes 2621440 | tf_op jit(solution)/shard_map/new_rows/pallas_call | solution.py:360
  178.0 0.8 collective-permute-start.12
  179.4 2.2 collective-permute-start.14
  181.6 1.3 collective-permute-done.4.refs_5_.refs_2_
  182.8 3.4 %collective-permute-done.5.refs_6_.refs_3_ = bf16[2112,128]{1,0:T(8,128)(2,1)S(1)} collective-permute-done((bf16[2112,128]{1,0:T(8,128)(2,1)}, bf16[2112,128]{1,0:T(8,128)(2,1)S(1)}, u32[]{:S(2)}, u32[]{:S(2)}) %collective-permute-start.5) | collective-permute-done | bytes 540704 | tf_op jit(solution)/shard_map/ppermute | solution.py:458
  186.2 0.8 copy-done.3
  187.0 11.7 %new_rows.7.refs_0_ = bf16[1056,128]{1,0:T(8,128)(2,1)} custom-call(s32[1]{0:T(128)} %bitcast.4.refs_0_, bf16[8192,128]{1,0:T(8,128)(2,1)} %all-gather.2.cloned.1.call-done.refs_1_, f32[1,8192]{1,0:T(1,128)} %join_stats.1.refs_2_, bf16[32768,128]{1,0:T(8,128)(2,1)} %refs_3_.9, bf16[2112,128]{1,0:T(8,128)(2,1)} %copy-done.1, bf16[2112,128]{1,0:T(8,128)(2,1)} %copy-done.2, ...), custom_call_target="tpu_custom_call" | custom-call | flops 6442450944 | bytes 2621440 | tf_op jit(solution)/shard_map/new_rows/pallas_call | solution.py:360
  198.7 0.8 collective-permute-start.6
  199.5 1.4 collective-permute-start.7
  200.9 1.3 collective-permute-start.8
  202.8 0.7 copy-done.8
  203.6 5.2 %placed_rows.2 = (f32[32768,128]{1,0:T(8,128)}, f32[256,128]{1,0:T(8,128)}) custom-call(s32[8]{0:T(128)} %pad_add_fusion.2.starts_ref, bf16[2112,128]{1,0:T(8,128)(2,1)} %get-tuple-element.12.refs_0_, bf16[2112,128]{1,0:T(8,128)(2,1)} %copy-done.1, bf16[2112,128]{1,0:T(8,128)(2,1)} %copy-done.2, ...), custom_call_target="tpu_custom_call", output_to_operand_aliasing={{0}: (9, {}), {1}: (10, {})} | custom-call | tf_op jit(solution)/shard_map/placed_rows/pallas_call | solution.py:410
  210.2 3.3 %placed_rows.3 = (f32[32768,128]{1,0:T(8,128)}, f32[256,128]{1,0:T(8,128)}) custom-call(s32[4]{0:T(128)} %get-tuple-element.27.starts_ref, bf16[1056,128]{1,0:T(8,128)(2,1)} %new_rows.7.refs_0_, bf16[1056,128]{1,0:T(8,128)(2,1)} %copy-done.9, bf16[1056,128]{1,0:T(8,128)(2,1)} %copy-done.10, ...), custom_call_target="tpu_custom_call", output_to_operand_aliasing={{0}: (5, {}), {1}: (6, {})} | custom-call | tf_op jit(solution)/shard_map/placed_rows/pallas_call | solution.py:410
  (51 shorter events, 5.8 us)
Async XLA Ops:
  7.2 66.8 %all-gather.2.cloned.1.call-start = ((), (), s32[]{:S(2)}) async-start(), calls=%async_computation.1 | async-start | bytes 2621440 | tf_op jit(solution)/shard_map/all_gather | solution.py:480
  57.4 14.2 %all-to-all-start = ((f32[32,1,2048]{2,1,0:T(1,128)}), f32[32,1,2048]{2,1,0:T(1,128)S(1)}, u32[]{:S(2)}, u32[]{:S(2)}) async-start(f32[32,1,2048]{2,1,0:T(1,128)} %row_stats.1), calls=%async_computation | async-start | bytes 524288 | tf_op jit(solution)/shard_map/all_to_all | solution.py:482
  94.5 26.3 %collective-permute-start = (bf16[2112,128]{1,0:T(8,128)(2,1)}, bf16[2112,128]{1,0:T(8,128)(2,1)S(1)}, u32[]{:S(2)}, u32[]{:S(2)}) collective-permute-start(bf16[2112,128]{1,0:T(8,128)(2,1)} %new_rows.5.refs_4_), channel_id=1, source_target_pairs={{8,0},{0,8},{24,16},{16,24},{9,1},{1,9},{25,17},{17,25},{10,2},{2,... | collective-permute-start | bytes 1622024 | tf_op jit(solution)/shard_map/ppermute | solution.py:458
  95.0 27.4 %collective-permute-start.1 = (bf16[2112,128]{1,0:T(8,128)(2,1)}, bf16[2112,128]{1,0:T(8,128)(2,1)S(1)}, u32[]{:S(2)}, u32[]{:S(2)}) collective-permute-start(bf16[2112,128]{1,0:T(8,128)(2,1)} %new_rows.5.refs_4_), channel_id=1, source_target_pairs={{16,0},{24,8},{0,16},{8,24},{17,1},{25,9},{1,17},{9,25},{18,2},{26... | collective-permute-start | bytes 1622024 | tf_op jit(solution)/shard_map/ppermute | solution.py:458
  95.9 26.6 %collective-permute-start.2 = (bf16[2112,128]{1,0:T(8,128)(2,1)}, bf16[2112,128]{1,0:T(8,128)(2,1)S(1)}, u32[]{:S(2)}, u32[]{:S(2)}) collective-permute-start(bf16[2112,128]{1,0:T(8,128)(2,1)} %new_rows.5.refs_4_), channel_id=1, source_target_pairs={{24,0},{16,8},{8,16},{0,24},{25,1},{17,9},{9,17},{1,25},{26,2},{18... | collective-permute-start | bytes 1622024 | tf_op jit(solution)/shard_map/ppermute | solution.py:458
  118.9 41.6 %collective-permute-start.10 = (bf16[2112,128]{1,0:T(8,128)(2,1)}, bf16[2112,128]{1,0:T(8,128)(2,1)S(1)}, u32[]{:S(2)}, u32[]{:S(2)}) collective-permute-start(bf16[2112,128]{1,0:T(8,128)(2,1)} %new_rows.8.refs_4_), channel_id=1, source_target_pairs={{16,0},{24,8},{0,16},{8,24},{17,1},{25,9},{1,17},{9,25},{18,2},{26... | collective-permute-start | bytes 1622024 | tf_op jit(solution)/shard_map/ppermute | solution.py:458
  119.4 43.3 %collective-permute-start.11 = (bf16[2112,128]{1,0:T(8,128)(2,1)}, bf16[2112,128]{1,0:T(8,128)(2,1)S(1)}, u32[]{:S(2)}, u32[]{:S(2)}) collective-permute-start(bf16[2112,128]{1,0:T(8,128)(2,1)} %new_rows.8.refs_4_), channel_id=1, source_target_pairs={{24,0},{16,8},{8,16},{0,24},{25,1},{17,9},{9,17},{1,25},{26,2},{18... | collective-permute-start | bytes 1622024 | tf_op jit(solution)/shard_map/ppermute | solution.py:458
  120.9 1.6 copy-start.13
  120.9 41.9 %collective-permute-start.9 = (bf16[2112,128]{1,0:T(8,128)(2,1)}, bf16[2112,128]{1,0:T(8,128)(2,1)S(1)}, u32[]{:S(2)}, u32[]{:S(2)}) collective-permute-start(bf16[2112,128]{1,0:T(8,128)(2,1)} %new_rows.8.refs_4_), channel_id=1, source_target_pairs={{8,0},{0,8},{24,16},{16,24},{9,1},{1,9},{25,17},{17,25},{10,2},{2,... | collective-permute-start | bytes 1622024 | tf_op jit(solution)/shard_map/ppermute | solution.py:458
  122.4 0.8 copy-start.14
  123.2 0.8 copy-start.15
  159.1 20.3 %collective-permute-start.3 = (bf16[2112,128]{1,0:T(8,128)(2,1)}, bf16[2112,128]{1,0:T(8,128)(2,1)S(1)}, u32[]{:S(2)}, u32[]{:S(2)}) collective-permute-start(bf16[2112,128]{1,0:T(8,128)(2,1)} %get-tuple-element.12.refs_0_), channel_id=1, source_target_pairs={{8,0},{0,8},{24,16},{16,24},{9,1},{1,9},{25,17},{17,25},{10,2},{2,... | collective-permute-start | bytes 1622024 | tf_op jit(solution)/shard_map/ppermute | solution.py:458
  159.9 22.9 %collective-permute-start.4 = (bf16[2112,128]{1,0:T(8,128)(2,1)}, bf16[2112,128]{1,0:T(8,128)(2,1)S(1)}, u32[]{:S(2)}, u32[]{:S(2)}) collective-permute-start(bf16[2112,128]{1,0:T(8,128)(2,1)} %get-tuple-element.12.refs_0_), channel_id=1, source_target_pairs={{16,0},{24,8},{0,16},{8,24},{17,1},{25,9},{1,17},{9,25},{18,2},{26... | collective-permute-start | bytes 1622024 | tf_op jit(solution)/shard_map/ppermute | solution.py:458
  160.5 2.2 copy-start.4
  160.5 25.7 %collective-permute-start.5 = (bf16[2112,128]{1,0:T(8,128)(2,1)}, bf16[2112,128]{1,0:T(8,128)(2,1)S(1)}, u32[]{:S(2)}, u32[]{:S(2)}) collective-permute-start(bf16[2112,128]{1,0:T(8,128)(2,1)} %get-tuple-element.12.refs_0_), channel_id=1, source_target_pairs={{24,0},{16,8},{8,16},{0,24},{25,1},{17,9},{9,17},{1,25},{26,2},{18... | collective-permute-start | bytes 1622024 | tf_op jit(solution)/shard_map/ppermute | solution.py:458
  162.7 0.8 copy-start.5
  162.7 1.0 copy-start.6
  178.0 22.9 %collective-permute-start.12 = (bf16[1056,128]{1,0:T(8,128)(2,1)}, bf16[1056,128]{1,0:T(8,128)(2,1)S(1)}, u32[]{:S(2)}, u32[]{:S(2)}) collective-permute-start(bf16[1056,128]{1,0:T(8,128)(2,1)} %get-tuple-element.15.refs_4_), channel_id=1, source_target_pairs={{8,0},{0,8},{24,16},{16,24},{9,1},{1,9},{25,17},{17,25},{10,2},{2,... | collective-permute-start | bytes 811016 | tf_op jit(solution)/shard_map/ppermute | solution.py:458
  178.8 24.0 %collective-permute-start.13 = (bf16[1056,128]{1,0:T(8,128)(2,1)}, bf16[1056,128]{1,0:T(8,128)(2,1)S(1)}, u32[]{:S(2)}, u32[]{:S(2)}) collective-permute-start(bf16[1056,128]{1,0:T(8,128)(2,1)} %get-tuple-element.15.refs_4_), channel_id=1, source_target_pairs={{16,0},{24,8},{0,16},{8,24},{17,1},{25,9},{1,17},{9,25},{18,2},{26... | collective-permute-start | bytes 811016 | tf_op jit(solution)/shard_map/ppermute | solution.py:458
  179.4 6.8 %copy-start.1 = (bf16[2112,128]{1,0:T(8,128)(2,1)}, bf16[2112,128]{1,0:T(8,128)(2,1)S(1)}, u32[]{:S(2)}) copy-start(bf16[2112,128]{1,0:T(8,128)(2,1)S(1)} %collective-permute-done.3.refs_4_.refs_1_) | copy-start | bytes 1622020
  179.4 23.4 %collective-permute-start.14 = (bf16[1056,128]{1,0:T(8,128)(2,1)}, bf16[1056,128]{1,0:T(8,128)(2,1)S(1)}, u32[]{:S(2)}, u32[]{:S(2)}) collective-permute-start(bf16[1056,128]{1,0:T(8,128)(2,1)} %get-tuple-element.15.refs_4_), channel_id=1, source_target_pairs={{24,0},{16,8},{8,16},{0,24},{25,1},{17,9},{9,17},{1,25},{26,2},{18... | collective-permute-start | bytes 811016 | tf_op jit(solution)/shard_map/ppermute | solution.py:458
  182.8 3.4 %copy-start.2 = (bf16[2112,128]{1,0:T(8,128)(2,1)}, bf16[2112,128]{1,0:T(8,128)(2,1)S(1)}, u32[]{:S(2)}) copy-start(bf16[2112,128]{1,0:T(8,128)(2,1)S(1)} %collective-permute-done.4.refs_5_.refs_2_) | copy-start | bytes 1622020
  186.2 0.8 copy-start.3
  198.7 10.1 %collective-permute-start.6 = (bf16[1056,128]{1,0:T(8,128)(2,1)}, bf16[1056,128]{1,0:T(8,128)(2,1)S(1)}, u32[]{:S(2)}, u32[]{:S(2)}) collective-permute-start(bf16[1056,128]{1,0:T(8,128)(2,1)} %new_rows.7.refs_0_), channel_id=1, source_target_pairs={{8,0},{0,8},{24,16},{16,24},{9,1},{1,9},{25,17},{17,25},{10,2},{2,... | collective-permute-start | bytes 811016 | tf_op jit(solution)/shard_map/ppermute | solution.py:458
  199.5 9.3 %collective-permute-start.7 = (bf16[1056,128]{1,0:T(8,128)(2,1)}, bf16[1056,128]{1,0:T(8,128)(2,1)S(1)}, u32[]{:S(2)}, u32[]{:S(2)}) collective-permute-start(bf16[1056,128]{1,0:T(8,128)(2,1)} %new_rows.7.refs_0_), channel_id=1, source_target_pairs={{16,0},{24,8},{0,16},{8,24},{17,1},{25,9},{1,17},{9,25},{18,2},{26... | collective-permute-start | bytes 811016 | tf_op jit(solution)/shard_map/ppermute | solution.py:458
  200.9 1.9 copy-start.7
  200.9 8.5 %collective-permute-start.8 = (bf16[1056,128]{1,0:T(8,128)(2,1)}, bf16[1056,128]{1,0:T(8,128)(2,1)S(1)}, u32[]{:S(2)}, u32[]{:S(2)}) collective-permute-start(bf16[1056,128]{1,0:T(8,128)(2,1)} %new_rows.7.refs_0_), channel_id=1, source_target_pairs={{24,0},{16,8},{8,16},{0,24},{25,1},{17,9},{9,17},{1,25},{26,2},{18... | collective-permute-start | bytes 811016 | tf_op jit(solution)/shard_map/ppermute | solution.py:458
  202.8 0.7 copy-start.8
  202.8 0.8 copy-start.11
  208.8 0.7 copy-start.9
  208.8 0.8 copy-start.10
  209.4 0.7 copy-start.12
  (1 other events, 0.7 us)
Sparse Core Ops, SparseCore 0:
  9.8 38.0 all-gather.1

commit v2 on v1

--- a/solution.py
+++ b/solution.py
@@ -251,7 +251,17 @@
     return block_rows + block_rows // 32
 
 
-def update_kernel(unread, pieces, block_rows, *refs):
+def combine(groups, parts_ref, out_ref):
+    per_group = parts_ref.shape[0] // groups
+    count = parts_ref.shape[2]
+    for t in range(groups):
+        parts = [parts_ref[t * per_group + k] for k in range(per_group)]
+        top = functools.reduce(jnp.maximum, parts)
+        total = functools.reduce(jnp.add, [jnp.exp(part - top) for part in parts])
+        out_ref[:, t * count : (t + 1) * count] = top + jnp.log(total)
+
+
+def update_kernel(joins, unread, pieces, block_rows, *refs):
     place_ref, tok_ref, lse_ref, cent_ref = refs[:4]
     refs = refs[4 + unread :]
     code_refs, refs = refs[: sum(pieces)], refs[sum(pieces) :]
@@ -264,6 +274,9 @@
         )
     else:
         code_ref, scratch, placing = refs[0], refs[1:], None
+    if joins:
+        parts_ref, lse_ref, scratch = lse_ref, scratch[0], scratch[1:]
+        pl.when(pl.program_id(0) == 0)(lambda: combine(joins, parts_ref, lse_ref))
     weights_ref, total_ref, mass_ref = scratch[:3]
     step, steps = pl.program_id(0), pl.num_programs(0)
     width = tok_ref.shape[1]
@@ -325,10 +338,10 @@
         pl.when(step == steps - 1)(placing.finish)
 
 
-def updated_chunk(block, toks, lse, centroids, blocks, block_rows, after=(), received=None):
+def updated_chunk(block, toks, lse, centroids, blocks, block_rows, after=(), received=None, joins=0):
     all_count, width = toks.shape
     depth = divisor(all_count, 2048)
-    tile = divisor(block_rows, 512)
+    tile = divisor(block_rows, 1024)
     rows = blocks * block_rows
     full = coded_rows(block_rows)
     anywhere = pl.BlockSpec(memory_space=pl.ANY)
@@ -336,7 +349,7 @@
     place, operands = block.reshape(1), [toks, lse, centroids, *after]
     in_specs = [
         pl.BlockSpec((all_count, width), whole),
-        pl.BlockSpec((1, all_count), whole),
+        pl.BlockSpec(lse.shape, (lambda j, place: (0, 0, 0)) if joins else whole),
         pl.BlockSpec((block_rows, width), lambda j, place: (place[0] + j, 0)),
     ] + [anywhere] * len(after)
     out_specs = [pl.BlockSpec((full, width), lambda j, place: (j, 0))]
@@ -347,6 +360,9 @@
         pltpu.VMEM((block_rows // 128, 128), jnp.float32),
     ]
     aliases, pieces = {}, []
+    if joins:
+        out_specs.append(pl.BlockSpec((1, all_count), whole))
+        out_shape.append(jax.ShapeDtypeStruct((1, all_count), jnp.float32))
     if received:
         codes, starts, outs = received
         pieces = [len(parts) for parts in codes]
@@ -358,7 +374,7 @@
         aliases = {len(operands) - 1: 1, len(operands): 2}
         scratch_shapes += Placing.scratch(len(codes), codes[0][0].shape[0] // full, block_rows, width)
     return pl.pallas_call(
-        functools.partial(update_kernel, len(after), pieces, block_rows),
+        functools.partial(update_kernel, joins, len(after), pieces, block_rows),
         grid_spec=pltpu.PrefetchScalarGridSpec(
             num_scalar_prefetch=1,
             grid=(blocks,),
@@ -368,7 +384,7 @@
         ),
         out_shape=out_shape,
         input_output_aliases=aliases,
-        compiler_params=pltpu.CompilerParams(vmem_limit_bytes=vmem_bytes),
+        compiler_params=pltpu.CompilerParams(vmem_limit_bytes=vmem_bytes * 3 // 4),
         cost_estimate=pl.CostEstimate(
             flops=6 * all_count * rows * width,
             bytes_accessed=(2 * all_count + 4 * rows) * width,
@@ -418,27 +434,9 @@
         ),
         out_shape=[jax.ShapeDtypeStruct(out.shape, out.dtype) for out in outs],
         input_output_aliases={1 + len(operands): 0, 2 + len(operands): 1},
-        compiler_params=pltpu.CompilerParams(vmem_limit_bytes=vmem_bytes),
+        compiler_params=pltpu.CompilerParams(vmem_limit_bytes=vmem_bytes // 2),
         name="placed_rows",
     )(jnp.concatenate(starts).astype(jnp.int32), *operands, *outs)
-
-
-def combine_kernel(groups, parts_ref, out_ref):
-    per_group = parts_ref.shape[0] // groups
-    count = parts_ref.shape[2]
-    for t in range(groups):
-        parts = [parts_ref[t * per_group + k] for k in range(per_group)]
-        top = functools.reduce(jnp.maximum, parts)
-        total = functools.reduce(jnp.add, [jnp.exp(part - top) for part in parts])
-        out_ref[:, t * count : (t + 1) * count] = top + jnp.log(total)
-
-
-def combined_lse(parts, groups):
-    return pl.pallas_call(
-        functools.partial(combine_kernel, groups),
-        out_shape=jax.ShapeDtypeStruct((1, groups * parts.shape[2]), jnp.float32),
-        name="join_stats",
-    )(parts)
 
 
 def blank(shape):
@@ -480,7 +478,6 @@
     toks = lax.all_gather(tokens, "tok", axis=0, tiled=True)
     own_lse = local_lse(tokens, centroids, tok_size * cent_size)
     parts = lax.all_to_all(own_lse, ("tok", "cent"), 0, 0, tiled=True)
-    lse = combined_lse(parts, tok_size)
 
     block_rows = divisor(share_rows, 1024)
     sources = jnp.stack([partner(me, s, tok_size) for s in range(tok_size)])
@@ -489,16 +486,18 @@
     plan = chunk_plan(share_rows // block_rows)
     for k, blocks in enumerate(plan):
         block = first * tok_size + me * blocks
-        after, received = (), None
-        if len(waiting) == 2:
-            if k + 1 < len(plan):
+        arrived, received = [], None
+        if len(waiting) > 1:
+            arrived = sum(waiting[-2][0][1:], [])
+            if blocks == 1:
                 received = (*waiting.pop(0), outs)
-            else:
-                after = sum(waiting[0][0][1:], [])
-        codes, *placed_outs = updated_chunk(
-            block, toks, lse, centroids, blocks, block_rows, after, received
-        )
-        outs = placed_outs or outs
+                arrived = arrived if waiting[1:] else []
+        operands = toks, lse if k else parts, centroids, blocks, block_rows, arrived, received
+        codes, *rest = updated_chunk(block, *operands, joins=0 if k else tok_size)
+        if not k:
+            (lse,) = rest
+        elif received:
+            outs = rest
         found = [[part] for part in from_others(codes, "tok")]
         waiting.append((found, first * tok_size + sources * blocks))
         first += blocks

time: 224 us -> 208 us (0.929)
  Pallas kernels: 162 us -> 138 us
  waiting for transfers between devices: 14.5 us -> 25.4 us
    pallas_call x6 -> x5, Pallas kernels: 104 us -> 81.8 us  [updated_chunk(): pl.pallas_call(functools.partial(update_kernel, joins, len(after), pieces...]
    ppermute x15, waiting for transfers between devices: 5.26 us -> 14.6 us  [from_others(): found.append(lax.ppermute(value, axis, pairs))]
    unnamed x32 -> x6, local copies, waits for them, and re-layouts: 5.62 us -> 4.98 us
  transfers between devices with their start and end apart: 17 -> 17, of which waited for: 4 -> 7; matrix products, arithmetic and copies ran while one was open for 1% -> 0% of each run, Pallas kernels for 63% -> 57%
where the time goes in v2:
time: 208 us; the launch traced here: 205 us
  Pallas kernels  138 us (66%)
  waiting for transfers between devices  25.4 us (12%)
  starting transfers between devices  21.8 us (10%)
  between operations  14.6 us (7%)
  local copies, waits for them, and re-layouts  4.98 us (2%)
    pallas_call x5, Pallas kernels, updated_chunk(): pl.pallas_call(functools.partial(update_kernel, joins, len(after), pieces...  81.8 us
    pallas_call x1, Pallas kernels, local_lse(): pl.pallas_call(functools.partial(stats_kernel, sub_rows, tok_cols), grid=...  49.5 us
    ppermute x15, starting transfers between devices, from_others(): found.append(lax.ppermute(value, axis, pairs))  17.8 us
    ppermute x15, waiting for transfers between devices, from_others(): found.append(lax.ppermute(value, axis, pairs))  14.6 us
    all_to_all x1, waiting for transfers between devices, local(): parts = lax.all_to_all(own_lse, ('tok', 'cent'), 0, 0, tiled=True)  10.1 us
    pallas_call x2, Pallas kernels, placed(): pl.pallas_call(functools.partial(place_kernel, chunks, block_rows), grid_...  6.76 us
    unnamed x6, local copies, waits for them, and re-layouts  4.98 us
  transfers between devices with their start and end apart: 17, of which 7 were waited for; matrix products, arithmetic and copies ran while one was open for 0% of the time, Pallas kernels for 57%

profile of v2, /device:TPU:0, one launch (start us, length us, event | category | flops | bytes accessed | tf_op | source)
XLA Modules:
  0.0 205.1 jit_solution(1243675163962215703)
XLA Ops:
  7.2 0.7 all-gather.2.cloned.1.call-update
  7.9 49.5 %row_stats.1 = f32[32,1,2048]{2,1,0:T(1,128)} custom-call(bf16[2048,128]{1,0:T(8,128)(2,1)} %tok_ref.1, bf16[32768,128]{1,0:T(8,128)(2,1)} %refs_3_.9), custom_call_target="tpu_custom_call" | custom-call | flops 17179869184 | bytes 8912896 | tf_op jit(solution)/shard_map/row_stats/pallas_call | solution.py:140
  57.4 3.9 %all-to-all-start = ((f32[32,1,2048]{2,1,0:T(1,128)}), f32[32,1,2048]{2,1,0:T(1,128)S(1)}, u32[]{:S(2)}, u32[]{:S(2)}) async-start(f32[32,1,2048]{2,1,0:T(1,128)} %row_stats.1), calls=%async_computation | async-start | bytes 524288 | tf_op jit(solution)/shard_map/all_to_all | solution.py:480
  61.6 10.1 %all-to-all-done.refs_2_ = f32[32,1,2048]{2,1,0:T(1,128)S(1)} async-done(((f32[32,1,2048]{2,1,0:T(1,128)}), f32[32,1,2048]{2,1,0:T(1,128)S(1)}, u32[]{:S(2)}, u32[]{:S(2)}) %all-to-all-start) | async-done | bytes 262176 | tf_op jit(solution)/shard_map/all_to_all | solution.py:480
  71.7 3.4 %copy-done = bf16[32768,128]{1,0:T(8,128)(2,1)S(1)} copy-done((bf16[32768,128]{1,0:T(8,128)(2,1)S(1)}, bf16[32768,128]{1,0:T(8,128)(2,1)}, u32[]{:S(2)}) %copy-start) | copy-done | bytes 8388632
  75.1 1.6 copy-done.1
  76.7 18.2 %new_rows.5 = (bf16[2112,128]{1,0:T(8,128)(2,1)S(1)}, f32[1,8192]{1,0:T(1,128)S(1)}) custom-call(s32[1]{0:T(128)} %bitcast.5.refs_0_, bf16[8192,128]{1,0:T(8,128)(2,1)S(1)} %copy-done.1, f32[32,1,2048]{2,1,0:T(1,128)S(1)} %all-to-all-done.refs_2_, bf16[32768,128]{1,0:T(8,128)(2,1)S(1)} %copy-done), custom_call_target="tpu_custom_call" | custom-call | flops 12884901888 | bytes 3145728 | tf_op jit(solution)/shard_map/new_rows/pallas_call | solution.py:376
  94.9 0.6 collective-permute-start
  95.5 0.8 collective-permute-start.1
  96.3 2.2 %collective-permute-start.2 = (bf16[2112,128]{1,0:T(8,128)(2,1)S(1)}, bf16[2112,128]{1,0:T(8,128)(2,1)S(1)}, u32[]{:S(2)}, u32[]{:S(2)}) collective-permute-start(bf16[2112,128]{1,0:T(8,128)(2,1)S(1)} %get-tuple-element.15.refs_7_), channel_id=1, source_target_pairs={{24,0},{16,8},{8,16},{0,24},{25,1},{17,9},{9,17},{1,25},{26,2},{18... | collective-permute-start | bytes 1622024 | tf_op jit(solution)/shard_map/ppermute | solution.py:456
  98.5 18.7 %new_rows.7.refs_7_ = bf16[2112,128]{1,0:T(8,128)(2,1)S(1)} custom-call(s32[1]{0:T(128)} %bitcast.7.refs_0_, bf16[8192,128]{1,0:T(8,128)(2,1)S(1)} %copy-done.2, f32[1,8192]{1,0:T(1,128)S(1)} %get-tuple-element.14.refs_2_, bf16[32768,128]{1,0:T(8,128)(2,1)S(1)} %copy-done), custom_call_target="tpu_custom_call" | custom-call | flops 12884901888 | bytes 3145728 | tf_op jit(solution)/shard_map/new_rows/pallas_call | solution.py:376
  117.2 0.5 collective-permute-start.6
  117.7 0.8 collective-permute-start.7
  118.6 2.2 %collective-permute-start.8 = (bf16[2112,128]{1,0:T(8,128)(2,1)S(1)}, bf16[2112,128]{1,0:T(8,128)(2,1)S(1)}, u32[]{:S(2)}, u32[]{:S(2)}) collective-permute-start(bf16[2112,128]{1,0:T(8,128)(2,1)S(1)} %new_rows.7.refs_7_), channel_id=1, source_target_pairs={{24,0},{16,8},{8,16},{0,24},{25,1},{17,9},{9,17},{1,25},{26,2},{18... | collective-permute-start | bytes 1622024 | tf_op jit(solution)/shard_map/ppermute | solution.py:456
  120.8 1.1 collective-permute-done.1.refs_5_.refs_9_
  121.8 19.3 %new_rows.6.refs_0_ = bf16[2112,128]{1,0:T(8,128)(2,1)S(1)} custom-call(s32[1]{0:T(128)} %bitcast.6.refs_0_, bf16[8192,128]{1,0:T(8,128)(2,1)S(1)} %copy-done.2, f32[1,8192]{1,0:T(1,128)S(1)} %get-tuple-element.14.refs_2_, bf16[32768,128]{1,0:T(8,128)(2,1)} %refs_3_.9, bf16[2112,128]{1,0:T(8,128)(2,1)S(1)} %collective-permute-done.refs_4_.refs_8_, ...), custom_call_target="tpu_custom_call" | custom-call | flops 12884901888 | bytes 3145728 | tf_op jit(solution)/shard_map/new_rows/pallas_call | solution.py:376
  141.1 1.9 collective-permute-start.3
  143.3 1.4 collective-permute-start.5
  145.0 12.8 %new_rows.8 = (bf16[1056,128]{1,0:T(8,128)(2,1)S(1)}, f32[32768,128]{1,0:T(8,128)}, f32[256,128]{1,0:T(8,128)}) custom-call(s32[5]{0:T(128)S(1)} %pad_add_fusion.2.refs_0_, bf16[8192,128]{1,0:T(8,128)(2,1)S(1)} %copy-done.2, f32[1,8192]{1,0:T(1,128)S(1)} %get-tuple-element.14.refs_2_, ...), custom_call_target="tpu_custom_call", output_to_operand_aliasing={{1}: (11, {}), {2}: (12, {})} | custom-call | flops 6442450944 | bytes 2621440 | tf_op jit(solution)/shard_map/new_rows/pallas_call | solution.py:376
  157.8 1.8 collective-permute-start.12
  159.6 0.3 collective-permute-start.13
  159.9 1.4 collective-permute-start.14
  161.4 6.0 %collective-permute-done.4.refs_5_.refs_2_ = bf16[2112,128]{1,0:T(8,128)(2,1)S(1)} collective-permute-done((bf16[2112,128]{1,0:T(8,128)(2,1)S(1)}, bf16[2112,128]{1,0:T(8,128)(2,1)S(1)}, u32[]{:S(2)}, u32[]{:S(2)}) %collective-permute-start.4) | collective-permute-done | bytes 540704 | tf_op jit(solution)/shard_map/ppermute | solution.py:456
  167.4 1.4 collective-permute-done.5.refs_6_.refs_3_
  168.8 12.8 %new_rows.9 = (bf16[1056,128]{1,0:T(8,128)(2,1)S(1)}, f32[32768,128]{1,0:T(8,128)}, f32[256,128]{1,0:T(8,128)}) custom-call(s32[5]{0:T(128)S(1)} %pad_add_fusion.1.refs_0_, bf16[8192,128]{1,0:T(8,128)(2,1)S(1)} %copy-done.2, f32[1,8192]{1,0:T(1,128)S(1)} %get-tuple-element.14.refs_2_, ...), custom_call_target="tpu_custom_call", output_to_operand_aliasing={{1}: (11, {}), {2}: (12, {})} | custom-call | flops 6442450944 | bytes 2621440 | tf_op jit(solution)/shard_map/new_rows/pallas_call | solution.py:376
  181.6 0.8 collective-permute-start.10
  182.5 1.8 collective-permute-start.11
  184.3 0.9 collective-permute-start.9
  185.3 4.4 %placed_rows.2 = (f32[32768,128]{1,0:T(8,128)}, f32[256,128]{1,0:T(8,128)}) custom-call(s32[8]{0:T(128)S(1)} %pad_add_fusion.3.starts_ref, bf16[2112,128]{1,0:T(8,128)(2,1)S(1)} %new_rows.6.refs_0_, bf16[2112,128]{1,0:T(8,128)(2,1)S(1)} %collective-permute-done.3.refs_4_.refs_1_, ...), custom_call_target="tpu_custom_call", output_to_operand_aliasing={{0}: (9, {}), {1}: (10, {})} | custom-call | tf_op jit(solution)/shard_map/placed_rows/pallas_call | solution.py:426
  189.7 4.5 %collective-permute-done.10.refs_2_ = bf16[1056,128]{1,0:T(8,128)(2,1)S(1)} collective-permute-done((bf16[1056,128]{1,0:T(8,128)(2,1)S(1)}, bf16[1056,128]{1,0:T(8,128)(2,1)S(1)}, u32[]{:S(2)}, u32[]{:S(2)}) %collective-permute-start.10) | collective-permute-done | bytes 270368 | tf_op jit(solution)/shard_map/ppermute | solution.py:456
  194.2 1.2 collective-permute-done.9.refs_1_
  195.4 2.4 %placed_rows.3 = (f32[32768,128]{1,0:T(8,128)}, f32[256,128]{1,0:T(8,128)}) custom-call(s32[4]{0:T(128)S(1)} %get-tuple-element.31.starts_ref, bf16[1056,128]{1,0:T(8,128)(2,1)S(1)} %get-tuple-element.18.refs_0_, bf16[1056,128]{1,0:T(8,128)(2,1)S(1)} %collective-permute-done.9.refs_1_, ...), custom_call_target="tpu_custom_call", output_to_operand_aliasing={{0}: (5, {}), {1}: (6, {})} | custom-call | tf_op jit(solution)/shard_map/placed_rows/pallas_call | solution.py:426
  (24 shorter events, 1.0 us)
Async XLA Ops:
  7.2 64.5 %all-gather.2.cloned.1.call-start = ((), (), s32[]{:S(2)}) async-start(), calls=%async_computation.1 | async-start | bytes 2621440 | tf_op jit(solution)/shard_map/all_gather | solution.py:478
  57.4 14.3 %all-to-all-start = ((f32[32,1,2048]{2,1,0:T(1,128)}), f32[32,1,2048]{2,1,0:T(1,128)S(1)}, u32[]{:S(2)}, u32[]{:S(2)}) async-start(f32[32,1,2048]{2,1,0:T(1,128)} %row_stats.1), calls=%async_computation | async-start | bytes 524288 | tf_op jit(solution)/shard_map/all_to_all | solution.py:480
  71.7 3.4 %copy-start = (bf16[32768,128]{1,0:T(8,128)(2,1)S(1)}, bf16[32768,128]{1,0:T(8,128)(2,1)}, u32[]{:S(2)}) copy-start(bf16[32768,128]{1,0:T(8,128)(2,1)} %refs_3_.9) | copy-start | bytes 25165828
  75.1 1.6 copy-start.1
  76.7 21.8 %copy-start.2 = (bf16[8192,128]{1,0:T(8,128)(2,1)S(1)}, bf16[8192,128]{1,0:T(8,128)(2,1)}, u32[]{:S(2)}) copy-start(bf16[8192,128]{1,0:T(8,128)(2,1)} %all-gather.2.cloned.1.call-done.refs_1_) | copy-start | bytes 6291460
  94.9 23.7 %collective-permute-start = (bf16[2112,128]{1,0:T(8,128)(2,1)S(1)}, bf16[2112,128]{1,0:T(8,128)(2,1)S(1)}, u32[]{:S(2)}, u32[]{:S(2)}) collective-permute-start(bf16[2112,128]{1,0:T(8,128)(2,1)S(1)} %get-tuple-element.15.refs_7_), channel_id=1, source_target_pairs={{8,0},{0,8},{24,16},{16,24},{9,1},{1,9},{25,17},{17,25},{10,2},{2,... | collective-permute-start | bytes 1622024 | tf_op jit(solution)/shard_map/ppermute | solution.py:456
  95.5 26.3 %collective-permute-start.1 = (bf16[2112,128]{1,0:T(8,128)(2,1)S(1)}, bf16[2112,128]{1,0:T(8,128)(2,1)S(1)}, u32[]{:S(2)}, u32[]{:S(2)}) collective-permute-start(bf16[2112,128]{1,0:T(8,128)(2,1)S(1)} %get-tuple-element.15.refs_7_), channel_id=1, source_target_pairs={{16,0},{24,8},{0,16},{8,24},{17,1},{25,9},{1,17},{9,25},{18,2},{26... | collective-permute-start | bytes 1622024 | tf_op jit(solution)/shard_map/ppermute | solution.py:456
  96.3 25.5 %collective-permute-start.2 = (bf16[2112,128]{1,0:T(8,128)(2,1)S(1)}, bf16[2112,128]{1,0:T(8,128)(2,1)S(1)}, u32[]{:S(2)}, u32[]{:S(2)}) collective-permute-start(bf16[2112,128]{1,0:T(8,128)(2,1)S(1)} %get-tuple-element.15.refs_7_), channel_id=1, source_target_pairs={{24,0},{16,8},{8,16},{0,24},{25,1},{17,9},{9,17},{1,25},{26,2},{18... | collective-permute-start | bytes 1622024 | tf_op jit(solution)/shard_map/ppermute | solution.py:456
  117.2 26.1 %collective-permute-start.6 = (bf16[2112,128]{1,0:T(8,128)(2,1)S(1)}, bf16[2112,128]{1,0:T(8,128)(2,1)S(1)}, u32[]{:S(2)}, u32[]{:S(2)}) collective-permute-start(bf16[2112,128]{1,0:T(8,128)(2,1)S(1)} %new_rows.7.refs_7_), channel_id=1, source_target_pairs={{8,0},{0,8},{24,16},{16,24},{9,1},{1,9},{25,17},{17,25},{10,2},{2,... | collective-permute-start | bytes 1622024 | tf_op jit(solution)/shard_map/ppermute | solution.py:456
  117.7 27.3 %collective-permute-start.7 = (bf16[2112,128]{1,0:T(8,128)(2,1)S(1)}, bf16[2112,128]{1,0:T(8,128)(2,1)S(1)}, u32[]{:S(2)}, u32[]{:S(2)}) collective-permute-start(bf16[2112,128]{1,0:T(8,128)(2,1)S(1)} %new_rows.7.refs_7_), channel_id=1, source_target_pairs={{16,0},{24,8},{0,16},{8,24},{17,1},{25,9},{1,17},{9,25},{18,2},{26... | collective-permute-start | bytes 1622024 | tf_op jit(solution)/shard_map/ppermute | solution.py:456
  118.6 26.4 %collective-permute-start.8 = (bf16[2112,128]{1,0:T(8,128)(2,1)S(1)}, bf16[2112,128]{1,0:T(8,128)(2,1)S(1)}, u32[]{:S(2)}, u32[]{:S(2)}) collective-permute-start(bf16[2112,128]{1,0:T(8,128)(2,1)S(1)} %new_rows.7.refs_7_), channel_id=1, source_target_pairs={{24,0},{16,8},{8,16},{0,24},{25,1},{17,9},{9,17},{1,25},{26,2},{18... | collective-permute-start | bytes 1622024 | tf_op jit(solution)/shard_map/ppermute | solution.py:456
  141.1 18.8 %collective-permute-start.3 = (bf16[2112,128]{1,0:T(8,128)(2,1)S(1)}, bf16[2112,128]{1,0:T(8,128)(2,1)S(1)}, u32[]{:S(2)}, u32[]{:S(2)}) collective-permute-start(bf16[2112,128]{1,0:T(8,128)(2,1)S(1)} %new_rows.6.refs_0_), channel_id=1, source_target_pairs={{8,0},{0,8},{24,16},{16,24},{9,1},{1,9},{25,17},{17,25},{10,2},{2,... | collective-permute-start | bytes 1622024 | tf_op jit(solution)/shard_map/ppermute | solution.py:456
  143.0 24.4 %collective-permute-start.4 = (bf16[2112,128]{1,0:T(8,128)(2,1)S(1)}, bf16[2112,128]{1,0:T(8,128)(2,1)S(1)}, u32[]{:S(2)}, u32[]{:S(2)}) collective-permute-start(bf16[2112,128]{1,0:T(8,128)(2,1)S(1)} %new_rows.6.refs_0_), channel_id=1, source_target_pairs={{16,0},{24,8},{0,16},{8,24},{17,1},{25,9},{1,17},{9,25},{18,2},{26... | collective-permute-start | bytes 1622024 | tf_op jit(solution)/shard_map/ppermute | solution.py:456
  143.3 25.5 %collective-permute-start.5 = (bf16[2112,128]{1,0:T(8,128)(2,1)S(1)}, bf16[2112,128]{1,0:T(8,128)(2,1)S(1)}, u32[]{:S(2)}, u32[]{:S(2)}) collective-permute-start(bf16[2112,128]{1,0:T(8,128)(2,1)S(1)} %new_rows.6.refs_0_), channel_id=1, source_target_pairs={{24,0},{16,8},{8,16},{0,24},{25,1},{17,9},{9,17},{1,25},{26,2},{18... | collective-permute-start | bytes 1622024 | tf_op jit(solution)/shard_map/ppermute | solution.py:456
  157.8 26.5 %collective-permute-start.12 = (bf16[1056,128]{1,0:T(8,128)(2,1)S(1)}, bf16[1056,128]{1,0:T(8,128)(2,1)S(1)}, u32[]{:S(2)}, u32[]{:S(2)}) collective-permute-start(bf16[1056,128]{1,0:T(8,128)(2,1)S(1)} %get-tuple-element.19.refs_4_), channel_id=1, source_target_pairs={{8,0},{0,8},{24,16},{16,24},{9,1},{1,9},{25,17},{17,25},{10,2},{2,... | collective-permute-start | bytes 811016 | tf_op jit(solution)/shard_map/ppermute | solution.py:456
  159.6 25.7 %collective-permute-start.13 = (bf16[1056,128]{1,0:T(8,128)(2,1)S(1)}, bf16[1056,128]{1,0:T(8,128)(2,1)S(1)}, u32[]{:S(2)}, u32[]{:S(2)}) collective-permute-start(bf16[1056,128]{1,0:T(8,128)(2,1)S(1)} %get-tuple-element.19.refs_4_), channel_id=1, source_target_pairs={{16,0},{24,8},{0,16},{8,24},{17,1},{25,9},{1,17},{9,25},{18,2},{26... | collective-permute-start | bytes 811016 | tf_op jit(solution)/shard_map/ppermute | solution.py:456
  159.9 25.3 %collective-permute-start.14 = (bf16[1056,128]{1,0:T(8,128)(2,1)S(1)}, bf16[1056,128]{1,0:T(8,128)(2,1)S(1)}, u32[]{:S(2)}, u32[]{:S(2)}) collective-permute-start(bf16[1056,128]{1,0:T(8,128)(2,1)S(1)} %get-tuple-element.19.refs_4_), channel_id=1, source_target_pairs={{24,0},{16,8},{8,16},{0,24},{25,1},{17,9},{9,17},{1,25},{26,2},{18... | collective-permute-start | bytes 811016 | tf_op jit(solution)/shard_map/ppermute | solution.py:456
  181.6 12.5 %collective-permute-start.10 = (bf16[1056,128]{1,0:T(8,128)(2,1)S(1)}, bf16[1056,128]{1,0:T(8,128)(2,1)S(1)}, u32[]{:S(2)}, u32[]{:S(2)}) collective-permute-start(bf16[1056,128]{1,0:T(8,128)(2,1)S(1)} %get-tuple-element.18.refs_0_), channel_id=1, source_target_pairs={{16,0},{24,8},{0,16},{8,24},{17,1},{25,9},{1,17},{9,25},{18,2},{26... | collective-permute-start | bytes 811016 | tf_op jit(solution)/shard_map/ppermute | solution.py:456
  182.5 11.7 %collective-permute-start.11 = (bf16[1056,128]{1,0:T(8,128)(2,1)S(1)}, bf16[1056,128]{1,0:T(8,128)(2,1)S(1)}, u32[]{:S(2)}, u32[]{:S(2)}) collective-permute-start(bf16[1056,128]{1,0:T(8,128)(2,1)S(1)} %get-tuple-element.18.refs_0_), channel_id=1, source_target_pairs={{24,0},{16,8},{8,16},{0,24},{25,1},{17,9},{9,17},{1,25},{26,2},{18... | collective-permute-start | bytes 811016 | tf_op jit(solution)/shard_map/ppermute | solution.py:456
  184.3 11.1 %collective-permute-start.9 = (bf16[1056,128]{1,0:T(8,128)(2,1)S(1)}, bf16[1056,128]{1,0:T(8,128)(2,1)S(1)}, u32[]{:S(2)}, u32[]{:S(2)}) collective-permute-start(bf16[1056,128]{1,0:T(8,128)(2,1)S(1)} %get-tuple-element.18.refs_0_), channel_id=1, source_target_pairs={{8,0},{0,8},{24,16},{16,24},{9,1},{1,9},{25,17},{17,25},{10,2},{2,... | collective-permute-start | bytes 811016 | tf_op jit(solution)/shard_map/ppermute | solution.py:456
Sparse Core Ops, SparseCore 0:
  9.8 38.0 all-gather.1
